TPU v7x, 32 devices: a whole 2x2x4 slice. The times are simulated.
32 devices in a mesh: ty: 4 (over z), tx: 8 (over y, x, core).
Axes of the slice: x: 2, y: 2, z: 4, core: 2. Of those that a mesh axis runs over, the one named last changes fastest.
Arguments:
- track_rows: float32 [16384, 2, 256], P(('ty', 'tx')), may hold values from -6 to 6
- track_tile: int32 [16384, 1], P(('ty', 'tx')), may hold values from 0 to 31; in each aligned block of 512 rows (0 to 511, 512 to 1023, ...) at most 32 rows name the same one
- track_slot: int32 [16384], P(('ty', 'tx')), may hold values from 0 to 2047
- velocity: float32 [2, 1024, 16384], P(None, 'ty', 'tx'), may hold values from -6 to 6
- viscosity: float32 [1024, 16384], P('ty', 'tx'), may hold values from 0.5 to 2
- log_friction: float32 [1024, 16384], P('ty', 'tx'), may hold values from -0.7 to 1.6
Outputs:
- adjoint: float32 [2, 1024, 16384], P(None, 'ty', 'tx')
- grad_slab: float32 [64, 1024], P(('ty', 'tx'))
Inputs may be any that keep to these rules, and one draw needn't show every extreme that they name: `track_tile`: among the 512 rows of one device at most 32 name the same tile, a bound that some block reaches.
All inputs are finite; a program needn't handle non-finite values.
Results may differ from a plain program's by a relative error of at most 0.00002.
Values sent between devices are 32-bit elements; how exact they have to be, the bound alone decides.
A program may use at most 128 MiB of HBM per device.

v0:
```python
import jax
import jax.numpy as jnp
from jax import lax
from jax.sharding import PartitionSpec as P

CB = 16
SWEEPS = 3


OMEGA = 0.8
CROSS_COUPLING = 3.0
REGULAR = 0.1


def padded_2(x, sides, width):
    for axis, dim in sides:
        count, length = (lax.axis_size(axis), x.shape[dim])
        up = [(i, (i + 1) % count) for i in range(count - 1)]
        down = [(j, i) for i, j in up]
        last = lax.slice_in_dim(x, length - width, length, axis=dim)
        first = lax.slice_in_dim(x, 0, width, axis=dim)
        before = lax.ppermute(last, axis, up)
        after = lax.ppermute(first, axis, down)
        x = jnp.concatenate([before, x, after], axis=dim)
    return x


def face_terms(eta_pad):
    central_stencil = eta_pad[1:-1, 1:-1]
    eastern_neighbor = 0.5 * (central_stencil + eta_pad[1:-1, 2:])
    western_neighbor = 0.5 * (central_stencil + eta_pad[1:-1, :-2])
    northern_neighbor = 0.5 * (central_stencil + eta_pad[2:, 1:-1])
    southern_neighbor = 0.5 * (central_stencil + eta_pad[:-2, 1:-1])
    return (
        central_stencil,
        eastern_neighbor,
        western_neighbor,
        northern_neighbor,
        southern_neighbor,
    )


def diagonal(eta_pad, friction_coeff):
    central_stencil, eastern_neighbor, western_neighbor, northern_neighbor, southern_neighbor = (
        face_terms(eta_pad)
    )
    diag_u = (
        4.0 * (eastern_neighbor + western_neighbor)
        + northern_neighbor
        + southern_neighbor
        + friction_coeff
    )
    diag_v = (
        4.0 * (northern_neighbor + southern_neighbor)
        + eastern_neighbor
        + western_neighbor
        + friction_coeff
    )
    return jnp.stack([diag_u, diag_v])


def mixed_derivative(field):
    return 0.25 * (field[2:, 2:] - field[2:, :-2] - field[:-2, 2:] + field[:-2, :-2])


def relax(multiplier_padded, force, eta_pad, friction_coeff):
    central_stencil, eastern_neighbor, western_neighbor, northern_neighbor, southern_neighbor = (
        face_terms(eta_pad)
    )
    u_padded_field = multiplier_padded[0]
    v_padded_field = multiplier_padded[1]
    u_interior = u_padded_field[1:-1, 1:-1]
    v_interior = v_padded_field[1:-1, 1:-1]
    apply_operator_u = (
        4.0
        * (
            eastern_neighbor * (u_interior - u_padded_field[1:-1, 2:])
            + western_neighbor * (u_interior - u_padded_field[1:-1, :-2])
        )
        + northern_neighbor * (u_interior - u_padded_field[2:, 1:-1])
        + southern_neighbor * (u_interior - u_padded_field[:-2, 1:-1])
        - CROSS_COUPLING * central_stencil * mixed_derivative(v_padded_field)
        + friction_coeff * u_interior
    )
    apply_operator_v = (
        4.0
        * (
            northern_neighbor * (v_interior - v_padded_field[2:, 1:-1])
            + southern_neighbor * (v_interior - v_padded_field[:-2, 1:-1])
        )
        + eastern_neighbor * (v_interior - v_padded_field[1:-1, 2:])
        + western_neighbor * (v_interior - v_padded_field[1:-1, :-2])
        - CROSS_COUPLING * central_stencil * mixed_derivative(u_padded_field)
        + friction_coeff * v_interior
    )
    return jnp.stack([u_interior, v_interior]) + OMEGA * (
        force - jnp.stack([apply_operator_u, apply_operator_v])
    ) / diagonal(eta_pad, friction_coeff)


def smoothing(q_pad):
    q_mid = q_pad[1:-1, 1:-1]
    return 4.0 * q_mid - (q_pad[1:-1, 2:] + q_pad[1:-1, :-2] + q_pad[2:, 1:-1] + q_pad[:-2, 1:-1])


def shards(track_rows, track_tile, track_slot, velocity, viscosity, log_friction):
    tile_rows, tile_cols = viscosity.shape
    tiles_y = lax.axis_size("ty")
    tiles_x = lax.axis_size("tx")
    devices = tiles_y * tiles_x
    rows_dev = track_rows.shape[0]
    seg_len = track_rows.shape[2]
    capacity = max(2, 2 * rows_dev // devices)
    slot_count = tile_rows * tile_cols // seg_len
    tile = track_tile[:, 0]
    onehot = (tile[:, None] == jnp.arange(devices, dtype=jnp.int32)[None, :]).astype(jnp.int32)
    before = jnp.cumsum(onehot, axis=0) - onehot
    rank = jnp.sum(before * onehot, axis=1)
    position = tile * capacity + rank
    send_rows = (
        jnp.zeros((devices * capacity, 2, seg_len), jnp.float32).at[position].set(track_rows)
    )
    send_slots = (
        jnp.zeros((devices * capacity,), jnp.float32)
        .at[position]
        .set(track_slot.astype(jnp.float32))
    )
    got_rows, got_slots = (
        lax.all_to_all(send_rows, ("ty", "tx"), split_axis=0, concat_axis=0, tiled=True),
        lax.all_to_all(send_slots, ("ty", "tx"), split_axis=0, concat_axis=0, tiled=True),
    )
    got_slots = got_slots.astype(jnp.int32)
    forcing = jnp.zeros((slot_count, 2, seg_len), jnp.float32).at[got_slots].add(got_rows)
    forcing = (
        forcing.reshape(tile_rows, tile_cols // seg_len, 2, seg_len)
        .transpose(2, 0, 1, 3)
        .reshape(2, tile_rows, tile_cols)
    )
    padded = padded_2(jnp.stack([viscosity, log_friction]), (("ty", 1), ("tx", 2)), 1)
    eta_pad = padded[0]
    q_pad = padded[1]
    friction_coeff = jnp.exp(log_friction)
    adjoint = OMEGA * forcing / diagonal(eta_pad, friction_coeff)
    for sweep in range(SWEEPS - 1):
        multiplier_padded = padded_2(adjoint, (("ty", 1), ("tx", 2)), 1)
        adjoint = relax(multiplier_padded, forcing, eta_pad, friction_coeff)
    gradient = -friction_coeff * (
        velocity[0] * adjoint[0] + velocity[1] * adjoint[1]
    ) + REGULAR * smoothing(q_pad)
    moved = lax.all_to_all(gradient, "tx", split_axis=0, concat_axis=1, tiled=True)
    grad_slab = moved.reshape(moved.shape[0] // CB, CB, moved.shape[1] // CB, CB).sum(axis=(1, 3))
    return (adjoint, grad_slab)


def solution(mesh):
    return jax.shard_map(
        shards,
        mesh=mesh,
        in_specs=(
            P(("ty", "tx"), None, None),
            P(("ty", "tx"), None),
            P(("ty", "tx")),
            P(None, "ty", "tx"),
            P("ty", "tx"),
            P("ty", "tx"),
        ),
        out_specs=(P(None, "ty", "tx"), P(("ty", "tx"), None)),
        check_vma=False,
    )
```

profile of v0, /device:TPU:0, one launch (start us, length us, event | category | flops | bytes accessed | tf_op | source)
XLA Modules:
  0.0 461.8 jit_solution(15964189707009443462)
XLA Ops:
  5.0 2.4 scatter_custom_fusion
  8.1 7.3 %all-to-all-start = ((f32[32,32,1]{1,2,0:T(1,128)}), f32[32,32,1]{1,2,0:T(1,128)S(1)}, u32[]{:S(2)}, u32[]{:S(2)}) async-start(f32[32,32,1]{1,2,0:T(1,128)} %bitcast.5), calls=%async_computation | async-start | bytes 32768 | tf_op jit(solution)/shard_map/all_to_all | solution.py:130
  15.4 1.9 broadcast_in_dim.15
  17.3 50.5 %scatter_fusion = f32[1024,2,256]{2,1,0:T(2,128)} fusion(f32[1024,2,256]{2,1,0:T(2,128)} %broadcast_in_dim.15, s32[512]{0:T(512)S(1)} %bitcast.86, f32[512,2,256]{2,1,0:T(2,128)S(1)} %copy-done.17), kind=kCustom, calls=%fused_computation.1 | custom fusion | bytes 3147776 | tf_op jit(solution)/shard_map/scatter | solution.py:121
  67.8 6.0 %all-to-all-start.1 = ((f32[1024,2,256]{2,1,0:T(2,128)}), f32[1024,2,256]{2,1,0:T(2,128)}, u32[]{:S(2)}, u32[]{:S(2)}) async-start(f32[1024,2,256]{2,1,0:T(2,128)} %scatter_fusion), calls=%async_computation.1 | async-start | bytes 4194304 | tf_op jit(solution)/shard_map/all_to_all | solution.py:129
  74.7 3.6 collective-permute-start
  78.3 1.3 collective-permute-start.1
  79.8 29.3 %collective-permute-done = f32[2,1,2048]{2,1,0:T(1,128)S(1)} collective-permute-done((f32[2,1,2048]{2,1,0:T(1,128)S(1)}, f32[2,1,2048]{2,1,0:T(1,128)S(1)}, u32[]{:S(2)}, u32[]{:S(2)}) %collective-permute-start) | collective-permute-done | bytes 16416 | tf_op jit(solution)/shard_map/ppermute | solution.py:22
  109.1 2.2 pad_maximum_fusion
  111.3 2.1 copy-done.12
  113.6 1.3 collective-permute-start.3
  114.9 3.0 collective-permute-start.2
  119.1 6.5 %concatenate.19 = f32[2,258,2050]{2,1,0:T(8,128)} concatenate(f32[2,258,1]{2,1,0:T(8,128)S(1)} %collective-permute-done.2, f32[2,258,2048]{2,1,0:T(8,128)} %copy-done.12, f32[2,258,1]{2,1,0:T(8,128)S(1)} %collective-permute-done.3), dimensions={2} | concatenate | bytes 8462400 | tf_op jit(solution)/shard_map/concatenate | solution.py:24
  125.6 4.2 slice_bitcast_fusion
  129.8 5.5 %add_bitcast_fusion.1 = (f32[1,256,2048]{2,1,0:T(8,128)}, f32[256,2048]{1,0:T(8,128)S(1)}, f32[256,2048]{1,0:T(8,128)}, f32[256,2048]{1,0:T(8,128)}, f32[256,2048]{1,0:T(8,128)}) fusion(f32[256,2048]{1,0:T(8,128)S(1)} %copy-done.1, f32[258,2050]{1,0:T(8,128)S(1)} %get-tuple-element.8), kind=kLoop, calls=%fused_computation.123 | loop fusion | flops 6815744 | bytes 23068672 | tf_op jit(solution)/shard_map/stack | solution.py:59
  135.3 1.3 copy-done.4
  136.6 5.3 %add_bitcast_fusion = f32[1,256,2048]{2,1,0:T(8,128)} fusion(f32[256,2048]{1,0:T(8,128)} %get-tuple-element.6, f32[256,2048]{1,0:T(8,128)} %get-tuple-element.5, f32[256,2048]{1,0:T(8,128)} %get-tuple-element.4, f32[256,2048]{1,0:T(8,128)S(1)} %get-tuple-element.3, f32[256,2048]{1,0:T(8,128)S(1)} %copy-done.1), kind=kLoop, calls=%fused_computation.122 | loop fusion | flops 2621440 | bytes 12582912 | tf_op jit(solution)/shard_map/stack | solution.py:59
  141.9 2.8 broadcast_in_dim.6
  144.8 128.3 %scatter_fusion.1 = f32[2048,2,256]{2,1,0:T(2,128)} fusion(f32[2048,2,256]{2,1,0:T(2,128)} %broadcast_in_dim.6, s32[1024]{0:T(1024)S(1)} %bitcast.83, f32[1024,2,256]{2,1,0:T(2,128)} %all-to-all-done.1), kind=kCustom, calls=%fused_computation.2 | custom fusion | flops 524288 | bytes 6295552 | tf_op jit(solution)/shard_map/scatter-add | solution.py:133
  273.0 4.5 copy.13
  277.5 4.9 %reshape.61 = f32[2,256,2048]{2,1,0:T(8,128)} reshape(f32[2,256,8,256]{3,2,1,0:T(8,128)} %copy.13) | data formatting | bytes 8388608 | tf_op jit(solution)/shard_map/reshape | solution.py:137
  282.4 4.3 multiply_divide_fusion
  286.8 8.8 %collective-permute-start.4 = (f32[2,1,2048]{2,1,0:T(1,128)S(1)}, f32[2,1,2048]{2,1,0:T(1,128)S(1)}, u32[]{:S(2)}, u32[]{:S(2)}) collective-permute-start(f32[2,1,2048]{2,1,0:T(1,128)S(1)} %get-tuple-element.21), channel_id=1, source_target_pairs={{0,8},{8,16},{16,24},{1,9},{9,17},{17,25},{2,10},{10,18},{18,26},{... | collective-permute-start | bytes 49160 | tf_op jit(solution)/shard_map/ppermute | solution.py:22
  295.6 1.3 collective-permute-start.5
  297.1 9.1 %collective-permute-done.5 = f32[2,1,2048]{2,1,0:T(1,128)S(1)} collective-permute-done((f32[2,1,2048]{2,1,0:T(1,128)S(1)}, f32[2,1,2048]{2,1,0:T(1,128)S(1)}, u32[]{:S(2)}, u32[]{:S(2)}) %collective-permute-start.5) | collective-permute-done | bytes 16416 | tf_op jit(solution)/shard_map/ppermute | solution.py:23
  306.6 2.0 copy-done.13
  308.8 1.3 collective-permute-start.7
  310.1 3.2 collective-permute-start.6
  314.3 6.5 %concatenate.21 = f32[2,258,2050]{2,1,0:T(8,128)} concatenate(f32[2,258,1]{2,1,0:T(8,128)S(1)} %collective-permute-done.6, f32[2,258,2048]{2,1,0:T(8,128)} %copy-done.13, f32[2,258,1]{2,1,0:T(8,128)S(1)} %collective-permute-done.7), dimensions={2} | concatenate | bytes 8462400 | tf_op jit(solution)/shard_map/concatenate | solution.py:24
  320.9 2.8 slice_bitcast_fusion.4
  325.7 6.5 %fusion.40 = f32[1,256,2048]{2,1,0:T(8,128)} fusion(f32[258,2050]{1,0:T(8,128)S(1)} %get-tuple-element.11, f32[256,2048]{1,0:T(8,128)} %get-tuple-element.6, f32[258,2050]{1,0:T(8,128)S(1)} %get-tuple-element.12, f32[256,2048]{1,0:T(8,128)S(1)} %copy-done.9, f32[256,2048]{1,0:T(8,128)S(1)} %copy-done.5, f32[256,2048]{1,0:T(8,128)S(1)} %copy-done.7, ...), kind=kLoop, calls=%fused_computation.79 | loop fusion | flops 11010048 | bytes 33554432 | tf_op jit(solution)/shard_map/stack | solution.py:97
  332.2 7.8 %fusion.53 = (f32[1,256,2048]{2,1,0:T(8,128)}, f32[1,256,2048]{2,1,0:T(8,128)}, f32[1,256,2048]{2,1,0:T(8,128)}) fusion(f32[258,2050]{1,0:T(8,128)S(1)} %get-tuple-element.12, f32[256,2048]{1,0:T(8,128)S(1)} %copy-done.5, f32[258,2050]{1,0:T(8,128)S(1)} %get-tuple-element.11, f32[256,2048]{1,0:T(8,128)S(1)} %copy-done.7, f32[256,2048]{1,0:T(8,128)} %get-tuple-element.6, ...), kind=kLoop, calls=%fused_computation.99 | loop fusion | flops 11010048 | bytes 39845888 | tf_op jit(solution)/shard_map/stack | solution.py:97
  340.0 6.6 %maximum_add_fusion = f32[2,256,2048]{2,1,0:T(8,128)S(1)} fusion(f32[1,256,2048]{2,1,0:T(8,128)} %get-tuple-element.30, f32[1,256,2048]{2,1,0:T(8,128)} %get-tuple-element.29, f32[2,256,2048]{2,1,0:T(8,128)} %reshape.61, f32[1,256,2048]{2,1,0:T(8,128)} %fusion.40, f32[1,256,2048]{2,1,0:T(8,128)} %get-tuple-element.28, f32[1,256,2048]{2,1,0:T(8,128)} %add_bitcast_fusion, ...), kind=kLoop, calls=%fused_computation.7 | loop fusion | flops 7340032 | bytes 20971520 | tf_op jit(solution)/shard_map/add | solution.py:96
  346.7 3.9 collective-permute-start.8
  350.6 1.3 collective-permute-start.9
  352.0 4.2 collective-permute-done.9
  356.7 2.0 copy-done.14
  358.9 1.3 collective-permute-start.11
  360.2 8.1 %collective-permute-start.10 = (f32[2,258,1]{2,1,0:T(8,128)S(1)}, f32[2,258,1]{2,1,0:T(8,128)S(1)}, u32[]{:S(2)}, u32[]{:S(2)}) collective-permute-start(f32[2,258,1]{2,1,0:T(8,128)S(1)} %get-tuple-element.14), channel_id=1, source_target_pairs={{0,1},{1,2},{2,3},{3,4},{4,5},{5,6},{6,7},{8,9},{9,10},{10,11},{11... | collective-permute-start | bytes 6200 | tf_op jit(solution)/shard_map/ppermute | solution.py:22
  369.3 6.5 %concatenate.23 = f32[2,258,2050]{2,1,0:T(8,128)} concatenate(f32[2,258,1]{2,1,0:T(8,128)S(1)} %collective-permute-done.10, f32[2,258,2048]{2,1,0:T(8,128)} %copy-done.14, f32[2,258,1]{2,1,0:T(8,128)S(1)} %collective-permute-done.11), dimensions={2} | concatenate | bytes 8462400 | tf_op jit(solution)/shard_map/concatenate | solution.py:24
  375.8 2.8 slice_bitcast_fusion.2
  380.6 6.5 %fusion.14 = f32[1,256,2048]{2,1,0:T(8,128)} fusion(f32[258,2050]{1,0:T(8,128)S(1)} %get-tuple-element.9, f32[256,2048]{1,0:T(8,128)} %get-tuple-element.6, f32[258,2050]{1,0:T(8,128)S(1)} %get-tuple-element.10, f32[256,2048]{1,0:T(8,128)S(1)} %copy-done.10, f32[256,2048]{1,0:T(8,128)S(1)} %copy-done.6, f32[256,2048]{1,0:T(8,128)S(1)} %copy-done.8, ...), kind=kLoop, calls=%fused_computation.39 | loop fusion | flops 11010048 | bytes 33554432 | tf_op jit(solution)/shard_map/stack | solution.py:97
  387.1 7.8 %fusion.27 = (f32[1,256,2048]{2,1,0:T(8,128)}, f32[1,256,2048]{2,1,0:T(8,128)}, f32[1,256,2048]{2,1,0:T(8,128)}) fusion(f32[258,2050]{1,0:T(8,128)S(1)} %get-tuple-element.10, f32[256,2048]{1,0:T(8,128)S(1)} %copy-done.6, f32[258,2050]{1,0:T(8,128)S(1)} %get-tuple-element.9, f32[256,2048]{1,0:T(8,128)S(1)} %copy-done.8, f32[256,2048]{1,0:T(8,128)} %get-tuple-element.6, ...), kind=kLoop, calls=%fused_computation.59 | loop fusion | flops 11010048 | bytes 39845888 | tf_op jit(solution)/shard_map/stack | solution.py:97
  394.9 6.8 %maximum_add_fusion.1 = f32[2,256,2048]{2,1,0:T(8,128)S(1)} fusion(f32[1,256,2048]{2,1,0:T(8,128)} %get-tuple-element.27, f32[1,256,2048]{2,1,0:T(8,128)} %get-tuple-element.26, f32[2,256,2048]{2,1,0:T(8,128)} %reshape.61, f32[1,256,2048]{2,1,0:T(8,128)} %fusion.14, f32[1,256,2048]{2,1,0:T(8,128)} %get-tuple-element.25, f32[1,256,2048]{2,1,0:T(8,128)} %add_bitcast_fusion, ...), kind=kLoop, calls=%fused_computation.11 | loop fusion | flops 7340032 | bytes 20971520 | tf_op jit(solution)/shard_map/add | solution.py:96
  402.7 2.5 fusion.6
  405.2 38.9 %all_to_all.30 = f32[8,32,2048]{2,1,0:T(8,128)S(1)} all-to-all(f32[8,32,2048]{2,1,0:T(8,128)S(1)} %bitcast.80), channel_id=1, replica_groups=mesh['ty'=4,'tx'=8] {'tx'}, dimensions={0} | all-to-all | bytes 4194304 | tf_op jit(solution)/shard_map/all_to_all | solution.py:150
  445.3 9.0 %reshape.62 = f32[2,16,1024,16]{3,2,1,0:T(8,128)} reshape(f32[32,8,2048]{2,1,0:T(8,128)S(1)} %copy.14) | data formatting | bytes 4194304 | tf_op jit(solution)/shard_map/reshape | solution.py:151
  454.3 7.5 %reduce_sum.22 = f32[2,1024]{1,0:T(2,128)} reduce(f32[2,16,1024,16]{3,2,1,0:T(8,128)} %reshape.62, f32[]{:T(128)} %constant.11.clone.1), dimensions={1,3}, to_apply=%region_6.7 | reduce | flops 522240 | bytes 2105348 | tf_op jit(solution)/shard_map/reduce_sum | solution.py:151
  (64 shorter events, 17.1 us)
Async XLA Ops:
  0.6 16.7 %copy-start.17 = (f32[512,2,256]{2,1,0:T(2,128)S(1)}, f32[512,2,256]{2,1,0:T(2,128)}, u32[]{:S(2)}) copy-start(f32[512,2,256]{2,1,0:T(2,128)} %param.6) | copy-start | bytes 3145732
  8.1 59.7 %all-to-all-start = ((f32[32,32,1]{1,2,0:T(1,128)}), f32[32,32,1]{1,2,0:T(1,128)S(1)}, u32[]{:S(2)}, u32[]{:S(2)}) async-start(f32[32,32,1]{1,2,0:T(1,128)} %bitcast.5), calls=%async_computation | async-start | bytes 32768 | tf_op jit(solution)/shard_map/all_to_all | solution.py:130
  67.8 6.0 %copy-start = (f32[256,2048]{1,0:T(8,128)S(1)}, f32[256,2048]{1,0:T(8,128)}, u32[]{:S(2)}) copy-start(f32[256,2048]{1,0:T(8,128)} %param.11) | copy-start | bytes 6291460
  67.8 74.1 %all-to-all-start.1 = ((f32[1024,2,256]{2,1,0:T(2,128)}), f32[1024,2,256]{2,1,0:T(2,128)}, u32[]{:S(2)}, u32[]{:S(2)}) async-start(f32[1024,2,256]{2,1,0:T(2,128)} %scatter_fusion), calls=%async_computation.1 | async-start | bytes 4194304 | tf_op jit(solution)/shard_map/all_to_all | solution.py:129
  74.7 34.4 %collective-permute-start = (f32[2,1,2048]{2,1,0:T(1,128)S(1)}, f32[2,1,2048]{2,1,0:T(1,128)S(1)}, u32[]{:S(2)}, u32[]{:S(2)}) collective-permute-start(f32[2,1,2048]{2,1,0:T(1,128)S(1)} %get-tuple-element.23), channel_id=1, source_target_pairs={{0,8},{8,16},{16,24},{1,9},{9,17},{17,25},{2,10},{10,18},{18,26},{... | collective-permute-start | bytes 49160 | tf_op jit(solution)/shard_map/ppermute | solution.py:22
  78.3 30.8 %collective-permute-start.1 = (f32[2,1,2048]{2,1,0:T(1,128)S(1)}, f32[2,1,2048]{2,1,0:T(1,128)S(1)}, u32[]{:S(2)}, u32[]{:S(2)}) collective-permute-start(f32[2,1,2048]{2,1,0:T(1,128)S(1)} %get-tuple-element.24), channel_id=1, source_target_pairs={{8,0},{16,8},{24,16},{9,1},{17,9},{25,17},{10,2},{18,10},{26,18},{... | collective-permute-start | bytes 49160 | tf_op jit(solution)/shard_map/ppermute | solution.py:23
  111.3 2.1 copy-start.12
  113.6 4.4 collective-permute-start.3
  114.9 4.2 collective-permute-start.2
  125.6 4.2 copy-start.1
  135.3 1.3 copy-start.4
  286.8 10.3 %collective-permute-start.4 = (f32[2,1,2048]{2,1,0:T(1,128)S(1)}, f32[2,1,2048]{2,1,0:T(1,128)S(1)}, u32[]{:S(2)}, u32[]{:S(2)}) collective-permute-start(f32[2,1,2048]{2,1,0:T(1,128)S(1)} %get-tuple-element.21), channel_id=1, source_target_pairs={{0,8},{8,16},{16,24},{1,9},{9,17},{17,25},{2,10},{10,18},{18,26},{... | collective-permute-start | bytes 49160 | tf_op jit(solution)/shard_map/ppermute | solution.py:22
  295.6 10.5 %collective-permute-start.5 = (f32[2,1,2048]{2,1,0:T(1,128)S(1)}, f32[2,1,2048]{2,1,0:T(1,128)S(1)}, u32[]{:S(2)}, u32[]{:S(2)}) collective-permute-start(f32[2,1,2048]{2,1,0:T(1,128)S(1)} %get-tuple-element.22), channel_id=1, source_target_pairs={{8,0},{16,8},{24,16},{9,1},{17,9},{25,17},{10,2},{18,10},{26,18},{... | collective-permute-start | bytes 49160 | tf_op jit(solution)/shard_map/ppermute | solution.py:23
  306.6 2.0 copy-start.13
  308.8 4.5 collective-permute-start.7
  310.1 4.2 collective-permute-start.6
  320.8 3.0 copy-start.2
  320.8 3.6 copy-start.5
  320.8 4.2 copy-start.7
  320.8 4.8 %copy-start.9 = (f32[256,2048]{1,0:T(8,128)S(1)}, f32[256,2048]{1,0:T(8,128)}, u32[]{:S(2)}) copy-start(f32[256,2048]{1,0:T(8,128)} %get-tuple-element.5) | copy-start | bytes 6291460
  346.7 5.4 %collective-permute-start.8 = (f32[2,1,2048]{2,1,0:T(1,128)S(1)}, f32[2,1,2048]{2,1,0:T(1,128)S(1)}, u32[]{:S(2)}, u32[]{:S(2)}) collective-permute-start(f32[2,1,2048]{2,1,0:T(1,128)S(1)} %get-tuple-element.19), channel_id=1, source_target_pairs={{0,8},{8,16},{16,24},{1,9},{9,17},{17,25},{2,10},{10,18},{18,26},{... | collective-permute-start | bytes 49160 | tf_op jit(solution)/shard_map/ppermute | solution.py:22
  350.6 5.6 %collective-permute-start.9 = (f32[2,1,2048]{2,1,0:T(1,128)S(1)}, f32[2,1,2048]{2,1,0:T(1,128)S(1)}, u32[]{:S(2)}, u32[]{:S(2)}) collective-permute-start(f32[2,1,2048]{2,1,0:T(1,128)S(1)} %get-tuple-element.20), channel_id=1, source_target_pairs={{8,0},{16,8},{24,16},{9,1},{17,9},{25,17},{10,2},{18,10},{26,18},{... | collective-permute-start | bytes 49160 | tf_op jit(solution)/shard_map/ppermute | solution.py:23
  356.7 2.0 copy-start.14
  358.9 9.4 %collective-permute-start.11 = (f32[2,258,1]{2,1,0:T(8,128)S(1)}, f32[2,258,1]{2,1,0:T(8,128)S(1)}, u32[]{:S(2)}, u32[]{:S(2)}) collective-permute-start(f32[2,258,1]{2,1,0:T(8,128)S(1)} %get-tuple-element.13), channel_id=1, source_target_pairs={{1,0},{2,1},{3,2},{4,3},{5,4},{6,5},{7,6},{9,8},{10,9},{11,10},{12... | collective-permute-start | bytes 6200 | tf_op jit(solution)/shard_map/ppermute | solution.py:23
  360.2 9.0 %collective-permute-start.10 = (f32[2,258,1]{2,1,0:T(8,128)S(1)}, f32[2,258,1]{2,1,0:T(8,128)S(1)}, u32[]{:S(2)}, u32[]{:S(2)}) collective-permute-start(f32[2,258,1]{2,1,0:T(8,128)S(1)} %get-tuple-element.14), channel_id=1, source_target_pairs={{0,1},{1,2},{2,3},{3,4},{4,5},{5,6},{6,7},{8,9},{9,10},{10,11},{11... | collective-permute-start | bytes 6200 | tf_op jit(solution)/shard_map/ppermute | solution.py:22
  375.8 3.0 copy-start.3
  375.8 3.6 copy-start.6
  375.8 4.2 copy-start.8
  375.8 4.8 %copy-start.10 = (f32[256,2048]{1,0:T(8,128)S(1)}, f32[256,2048]{1,0:T(8,128)}, u32[]{:S(2)}) copy-start(f32[256,2048]{1,0:T(8,128)} %get-tuple-element.5) | copy-start | bytes 6291460
  394.9 6.8 %copy-start.11 = (f32[258,2050]{1,0:T(8,128)S(1)}, f32[258,2050]{1,0:T(8,128)}, u32[]{:S(2)}) copy-start(f32[258,2050]{1,0:T(8,128)} %get-tuple-element.7) | copy-start | bytes 6346804
  394.9 7.7 %copy-start.16 = (f32[2,256,2048]{2,1,0:T(8,128)S(1)}, f32[2,256,2048]{2,1,0:T(8,128)}, u32[]{:S(2)}) copy-start(f32[2,256,2048]{2,1,0:T(8,128)} %param.9) | copy-start | bytes 12582916
  401.7 3.5 copy-start.15
where the time goes:
time: 470 us; the launch traced here: 462 us
  other arithmetic  204 us (43%)
  local copies, waits for them, and re-layouts  121 us (26%)
  starting transfers between devices  51.8 us (11%)
  waiting for transfers between devices  45.8 us (10%)
  blocking collectives  38.9 us (8%)
    scatter-add x1, other arithmetic, shards(): jnp.zeros((slot_count, 2, seg_len), jnp.float32).at[got_slots].add(got_rows)  128 us
    scatter x1, local copies, waits for them, and re-layouts, shards(): jnp.zeros((devices * capacity, 2, seg_len), jnp.float32).at[position]  50.5 us
    all_to_all x1, blocking collectives, shards(): lax.all_to_all(gradient, 'tx', split_axis=0, concat_axis=1, tiled=True)  38.9 us
    ppermute x6, waiting for transfers between devices, padded_2(): before = lax.ppermute(last, axis, up)  32.5 us
    ppermute x6, starting transfers between devices, padded_2(): before = lax.ppermute(last, axis, up)  30.7 us
    another operation x4, other arithmetic, relax(): jnp.stack([apply_operator_u, apply_operator_v])  28.6 us
    concatenate x3, local copies, waits for them, and re-layouts, padded_2(): x = jnp.concatenate([before, x, after], axis=dim)  19.6 us
    add x2, other arithmetic, relax(): jnp.stack([u_interior, v_interior])  13.4 us
  transfers between devices with their start and end apart: 14, of which 8 were waited for; matrix products, arithmetic and copies ran while one was open for 17% of the time, Pallas kernels for 0%

commit v1 on v0

v1 whole, which is shorter than its diff:
```python
import functools

import jax
import jax.numpy as jnp
from jax import lax
from jax.experimental import pallas as pl
from jax.experimental.pallas import tpu as pltpu
from jax.sharding import PartitionSpec as P

CB = 16
OMEGA = 0.8
REGULAR = 0.1
RH = 8
CH = 128
R0 = 16
VMEM_LIMIT = 56 * 1024 * 1024


def pack_kernel(cap, tile_ref, slot_ref, rows_ref, out_ref, count):
    devices = out_ref.shape[0]
    lanes = lax.broadcasted_iota(jnp.int32, (4, 128), 1)

    def clear(d, carry):
        count[d] = 0
        out_ref[d, cap] = jnp.zeros((4, 128), jnp.float32)
        return carry

    lax.fori_loop(0, devices, clear, 0)

    def place(i, carry):
        t = tile_ref[i]
        r = count[t]
        count[t] = r + 1
        out_ref[t, r] = rows_ref[i]
        slot = slot_ref[i].astype(jnp.float32)
        filled = (r + 1).astype(jnp.float32)
        head = out_ref[t, cap]
        out_ref[t, cap] = jnp.where(lanes == r, slot, jnp.where(lanes == cap, filled, head))
        return carry

    lax.fori_loop(0, rows_ref.shape[0], place, 0)


def scatter_kernel(cap, segs, meta_ref, got_ref, out_ref):
    out_ref[...] = jnp.zeros_like(out_ref)
    lanes = lax.broadcasted_iota(jnp.int32, (8, 128), 0)

    def source(s, carry):
        def add(r, inner):
            slot = meta_ref[s * 128 + r]
            y = slot // segs
            x = pl.multiple_of((slot % segs) * 256, 256)
            base = pl.multiple_of(y // 8 * 8, 8)
            chosen = lanes == y % 8
            spots = [(c, pl.ds(base, 8), pl.ds(x + 128 * h, 128)) for h in range(2) for c in range(2)]
            olds = [out_ref[spot] for spot in spots]
            news = [got_ref[s, r, pl.ds(j, 1), :] for j in range(4)]
            for spot, old, new in zip(spots, olds, news):
                out_ref[spot] = old + jnp.where(chosen, new, 0.0)
            return inner

        return lax.fori_loop(0, meta_ref[s * 128 + cap], add, carry)

    lax.fori_loop(0, got_ref.shape[0], source, 0)


def stencil_kernel(
    f_in, ft, fb, fl, fr, eta_in, q_in, et, eb, el, er, vel_in,
    adj_out, coarse_out,
    f, eta, q, a0, a1, inv, vel, gsum, sems,
):
    _, rows, cols = f_in.shape
    width = cols + 2 * CH
    ty, tx = lax.axis_index("ty"), lax.axis_index("tx")
    mid = (pl.ds(R0, rows), pl.ds(CH, cols))
    top = (pl.ds(R0 - RH, RH), pl.ds(CH, cols))
    bottom = (pl.ds(R0 + rows, RH), pl.ds(CH, cols))
    left = (pl.ds(R0 - RH, rows + 2 * RH), pl.ds(0, CH))
    right = (pl.ds(R0 - RH, rows + 2 * RH), pl.ds(CH + cols, CH))
    moves = []
    for i, (core, field) in enumerate(((eta_in, eta), (q_in, q))):
        moves.append((core, field.at[mid]))
        for edge, spot in ((et, top), (eb, bottom), (el, left), (er, right)):
            moves.append((edge.at[i], field.at[spot]))
    n_first = len(moves)
    for c in range(2):
        moves.append((f_in.at[c], f.at[(c,) + mid]))
        for edge, spot in ((ft, top), (fb, bottom), (fl, left), (fr, right)):
            moves.append((edge.at[c], f.at[(c,) + spot]))
    n_second = len(moves)
    moves.append((vel_in, vel))
    copies = [pltpu.make_async_copy(a, b, sems.at[i]) for i, (a, b) in enumerate(moves)]
    for copy in copies:
        copy.start()
    for copy in copies[:n_second]:
        copy.wait()

    def window(ref, start, *lead):
        return ref[lead + (pl.ds(start - 8, 24), slice(None))]

    def shifts(w):
        return w[9:17], w[7:15]

    def to_left(x):
        return pltpu.roll(x, width - 1, 1)

    def to_right(x):
        return pltpu.roll(x, 1, 1)

    def prepare(k, carry):
        start = pl.multiple_of(8 * k, 8)
        here = pl.ds(start, 8)
        w = window(eta, start)
        mine = w[8:16]
        nxt, prv = shifts(w)
        y_sum = nxt + prv
        x_sum = to_left(mine) + to_right(mine)
        base = 5.0 * mine + jnp.exp(q[here, :])
        inv_u = OMEGA / (base + 2.0 * x_sum + 0.5 * y_sum)
        inv_v = OMEGA / (base + 2.0 * y_sum + 0.5 * x_sum)
        inv[0, here, :] = inv_u
        inv[1, here, :] = inv_v
        a0[0, here, :] = inv_u * f[0, here, :]
        a0[1, here, :] = inv_v * f[1, here, :]
        return carry

    chunks = (rows + 2 * RH) // 8
    lax.fori_loop(1, 1 + chunks, prepare, 0)

    def sweep(src, start):
        here = pl.ds(start, 8)
        e = window(eta, start)
        u, v = window(src, start, 0), window(src, start, 1)
        gu, gv = e * u, e * v
        em, um, vm = e[8:16], u[8:16], v[8:16]
        gum, gvm = gu[8:16], gv[8:16]
        un, us = shifts(u)
        vn, vs = shifts(v)
        gun, gus = shifts(gu)
        gvn, gvs = shifts(gv)
        du, dv = 0.75 * (un - us), 0.75 * (vn - vs)
        u2, v2 = 2.0 * um, 0.5 * vm
        su = f[0, here, :] + em * (to_left(u2 + dv) + to_right(u2 - dv) + 0.5 * (un + us))
        su = su + 2.0 * (to_left(gum) + to_right(gum)) + 0.5 * (gun + gus)
        sv = f[1, here, :] + em * (to_left(v2 + du) + to_right(v2 - du) + 2.0 * (vn + vs))
        sv = sv + 0.5 * (to_left(gvm) + to_right(gvm)) + 2.0 * (gvn + gvs)
        keep = 1.0 - OMEGA
        return keep * um + inv[0, here, :] * su, keep * vm + inv[1, here, :] * sv

    def second(k, carry):
        start = pl.multiple_of(8 * k, 8)
        u, v = sweep(a0, start)
        a1[0, pl.ds(start, 8), :] = u
        a1[1, pl.ds(start, 8), :] = v
        return carry

    lax.fori_loop(1, 1 + chunks, second, 0)

    @pl.when(ty == 0)
    def _():
        a1[:, R0 - RH : R0, :] = jnp.zeros((2, RH, width), jnp.float32)

    @pl.when(ty == lax.axis_size("ty") - 1)
    def _():
        a1[:, R0 + rows : R0 + rows + RH, :] = jnp.zeros((2, RH, width), jnp.float32)

    @pl.when(tx == 0)
    def _():
        a1[:, :, :CH] = jnp.zeros((2, a1.shape[1], CH), jnp.float32)

    @pl.when(tx == lax.axis_size("tx") - 1)
    def _():
        a1[:, :, CH + cols :] = jnp.zeros((2, a1.shape[1], CH), jnp.float32)

    copies[-1].wait()
    inner = slice(CH, CH + cols)

    def third(k, carry):
        total = jnp.zeros((8, cols), jnp.float32)
        for half in range(CB // 8):
            own = pl.multiple_of(CB * k + 8 * half, 8)
            start = pl.multiple_of(own + R0, 8)
            u, v = sweep(a1, start)
            u, v = u[:, inner], v[:, inner]
            adj_out[0, pl.ds(own, 8), :] = u
            adj_out[1, pl.ds(own, 8), :] = v
            w = window(q, start)
            nxt, prv = shifts(w)
            mine = w[8:16]
            smooth = (4.0 * mine - (to_left(mine) + to_right(mine) + nxt + prv))[:, inner]
            data = vel[0, pl.ds(own, 8), :] * u + vel[1, pl.ds(own, 8), :] * v
            total = total + REGULAR * smooth - jnp.exp(mine[:, inner]) * data
        gsum[pl.ds(pl.multiple_of(8 * k, 8), 8), :] = total
        return carry

    lax.fori_loop(0, rows // CB, third, 0)
    sums = jnp.sum(gsum[...].reshape(rows // CB, 8, cols), axis=1)
    cell = lax.broadcasted_iota(jnp.int32, (cols, cols // CB), 0) // CB
    column = lax.broadcasted_iota(jnp.int32, (cols, cols // CB), 1)
    pick = (cell == column).astype(jnp.float32)
    coarse = jnp.dot(
        sums, pick, preferred_element_type=jnp.float32, precision=lax.Precision.HIGHEST
    )
    share = coarse_out.shape[1]
    for i in range(coarse_out.shape[0]):
        coarse_out[i] = coarse[i * share : (i + 1) * share]


def halos(x):
    rows, cols = x.shape[1:]

    def both(axis, last, first):
        up = [(i, i + 1) for i in range(lax.axis_size(axis) - 1)]
        down = [(j, i) for i, j in up]
        return lax.ppermute(last, axis, up), lax.ppermute(first, axis, down)

    top, bottom = both("ty", x[:, rows - RH :], x[:, :RH])

    def side(part):
        return jnp.concatenate([top[:, :, part], x[:, :, part], bottom[:, :, part]], axis=1)

    left, right = both("tx", side(slice(cols - CH, cols)), side(slice(0, CH)))
    return top, bottom, left, right


VMEM = pl.BlockSpec(memory_space=pltpu.VMEM)
SMEM = pl.BlockSpec(memory_space=pltpu.SMEM)
ANY = pl.BlockSpec(memory_space=pl.ANY)


def shards(track_rows, track_tile, track_slot, velocity, viscosity, log_friction):
    rows, cols = viscosity.shape
    tiles_x = lax.axis_size("tx")
    devices = lax.axis_size("ty") * tiles_x
    rows_dev, _, seg = track_rows.shape
    cap = max(2, 2 * rows_dev // devices)
    params = pltpu.CompilerParams(vmem_limit_bytes=VMEM_LIMIT)
    f32 = jnp.float32
    block = track_rows.reshape(rows_dev, 2, 2, 128).transpose(0, 2, 1, 3).reshape(rows_dev, 4, 128)
    packed = pl.pallas_call(
        functools.partial(pack_kernel, cap),
        out_shape=jax.ShapeDtypeStruct((devices, cap + 1, 4, 128), f32),
        in_specs=[SMEM, SMEM, VMEM],
        out_specs=VMEM,
        scratch_shapes=[pltpu.SMEM((devices,), jnp.int32)],
        compiler_params=params,
        name="pack",
    )(track_tile[:, 0], track_slot, block)
    got = lax.all_to_all(packed, ("ty", "tx"), split_axis=0, concat_axis=0, tiled=True)
    eq_halo = halos(jnp.stack([viscosity, log_friction]))
    meta = got[:, cap, 0, :].astype(jnp.int32).reshape(devices * 128)
    forcing = pl.pallas_call(
        functools.partial(scatter_kernel, cap, cols // seg),
        out_shape=jax.ShapeDtypeStruct((2, rows, cols), f32),
        in_specs=[SMEM, VMEM],
        out_specs=VMEM,
        compiler_params=params,
        name="scatter",
    )(meta, got)
    f_halo = halos(forcing)
    coarse_rows = rows // CB
    big = (rows + 2 * R0, cols + 2 * CH)
    adjoint, coarse = pl.pallas_call(
        stencil_kernel,
        out_shape=(
            jax.ShapeDtypeStruct((2, rows, cols), f32),
            jax.ShapeDtypeStruct((tiles_x, coarse_rows // tiles_x, cols // CB), f32),
        ),
        in_specs=[ANY] * 12,
        out_specs=(VMEM, VMEM),
        scratch_shapes=[
            pltpu.VMEM((2,) + big, f32),
            pltpu.VMEM(big, f32),
            pltpu.VMEM(big, f32),
            pltpu.VMEM((2,) + big, f32),
            pltpu.VMEM((2,) + big, f32),
            pltpu.VMEM((2,) + big, f32),
            pltpu.VMEM((2, rows, cols), f32),
            pltpu.VMEM((coarse_rows * 8, cols), f32),
            pltpu.SemaphoreType.DMA((21,)),
        ],
        compiler_params=params,
        name="stencil",
    )(forcing, *f_halo, viscosity, log_friction, *eq_halo, velocity)
    grad = lax.all_to_all(coarse, "tx", split_axis=0, concat_axis=2, tiled=True)
    return adjoint, grad[0]


def solution(mesh):
    return jax.shard_map(
        shards,
        mesh=mesh,
        in_specs=(
            P(("ty", "tx"), None, None),
            P(("ty", "tx"), None),
            P(("ty", "tx")),
            P(None, "ty", "tx"),
            P("ty", "tx"),
            P("ty", "tx"),
        ),
        out_specs=(P(None, "ty", "tx"), P(("ty", "tx"), None)),
        check_vma=False,
    )
```

time: 470 us -> 161 us (0.34); the launches traced: 462 us -> 161 us
  other arithmetic: 204 us -> 2.59 us
  local copies, waits for them, and re-layouts: 121 us -> 4 us
  Pallas kernels: 0 us -> 49.2 us
  blocking collectives: 38.9 us -> 16.3 us
  starting transfers between devices: 51.8 us -> 33.5 us
  waiting for transfers between devices: 45.8 us -> 54.6 us
    scatter-add x1 -> x0, other arithmetic: 128 us -> none  [shards(): jnp.zeros((slot_count, 2, seg_len), jnp.float32).at[got_slots].add(got_rows)]
    scatter x2 -> x0, local copies, waits for them, and re-layouts: 53 us -> none  [the longest x1 50.5 us: shards(): jnp.zeros((devices * capacity, 2, seg_len), jnp.float32).at[position]]
    pallas_call x0 -> x3, Pallas kernels: none -> 49.2 us  [the longest x1 29.1 us: shards(): pl.pallas_call(stencil_kernel, out_shape=(jax.ShapeDtypeStruct((2, rows,...]
    another operation x8 -> x0, other arithmetic: 40.6 us -> none  [the longest x4 28.6 us: relax(): jnp.stack([apply_operator_u, apply_operator_v])]
    all_to_all x1, blocking collectives: 38.9 us -> 16.3 us  [shards(): grad = lax.all_to_all(coarse, 'tx', split_axis=0, concat_axis=2, tiled=True)]
    concatenate x3 -> x0, local copies, waits for them, and re-layouts: 19.6 us -> none  [padded_2(): x = jnp.concatenate([before, x, after], axis=dim)]
    add x3 -> x0, other arithmetic: 15.9 us -> none  [the longest x2 13.4 us: relax(): jnp.stack([u_interior, v_interior])]
    reshape x2 -> x0, local copies, waits for them, and re-layouts: 13.9 us -> none  [the longest x1 9 us: shards(): moved.reshape(moved.shape[0] // CB, CB, moved.shape[1] // CB, CB)]
  transfers between devices with their start and end apart: 14 -> 9, of which waited for: 8 -> 6; matrix products, arithmetic and copies ran while one was open for 17% -> 3% of each run, Pallas kernels for 0% -> 7%
where the time goes in v1:
time: 161 us
  waiting for transfers between devices  54.6 us (34%)
  Pallas kernels  49.2 us (31%)
  starting transfers between devices  33.5 us (21%)
  blocking collectives  16.3 us (10%)
  local copies, waits for them, and re-layouts  4 us (2%)
  other arithmetic  2.59 us (2%)
    ppermute x8, waiting for transfers between devices, both(): return (lax.ppermute(last, axis, up), lax.ppermute(first, axis, down))  47.6 us
    pallas_call x1, Pallas kernels, shards(): pl.pallas_call(stencil_kernel, out_shape=(jax.ShapeDtypeStruct((2, rows,...  29.1 us
    ppermute x8, starting transfers between devices, both(): return (lax.ppermute(last, axis, up), lax.ppermute(first, axis, down))  26.1 us
    all_to_all x1, blocking collectives, shards(): grad = lax.all_to_all(coarse, 'tx', split_axis=0, concat_axis=2, tiled=True)  16.3 us
    pallas_call x1, Pallas kernels, shards(): pl.pallas_call(functools.partial(scatter_kernel, cap, cols // seg), out_s...  10.6 us
    pallas_call x1, Pallas kernels, shards(): pl.pallas_call(functools.partial(pack_kernel, cap), out_shape=jax.ShapeDt...  9.53 us
    all_to_all x1, starting transfers between devices, shards(): lax.all_to_all(packed, ('ty', 'tx'), split_axis=0, concat_axis=0, tiled=T...  7.41 us
    all_to_all x1, waiting for transfers between devices, shards(): lax.all_to_all(packed, ('ty', 'tx'), split_axis=0, concat_axis=0, tiled=T...  6.98 us
  transfers between devices with their start and end apart: 9, of which 6 were waited for; matrix products, arithmetic and copies ran while one was open for 3% of the time, Pallas kernels for 7%

profile of v1, /device:TPU:0, one launch (start us, length us, event | category | flops | bytes accessed | tf_op | source)
XLA Modules:
  0.0 161.1 jit_solution(7096366200430222499)
XLA Ops:
  0.6 9.5 %pack.1 = f32[32,33,4,128]{3,2,1,0:T(4,128)} custom-call(s32[512]{0:T(512)} %bitcast.21, s32[512]{0:T(512)} %slot_ref.1, f32[512,4,128]{2,1,0:T(4,128)} %bitcast.18), custom_call_target="tpu_custom_call" | custom-call | tf_op jit(solution)/shard_map/pack/pallas_call | solution.py:240
  10.2 0.0 copy-start
  10.2 7.4 %all-to-all-start = ((f32[32,33,4,128]{3,2,1,0:T(4,128)}), f32[32,33,4,128]{3,2,1,0:T(4,128)}, u32[]{:S(2)}, u32[]{:S(2)}) async-start(f32[32,33,4,128]{3,2,1,0:T(4,128)} %pack.1), calls=%async_computation | async-start | bytes 4325376 | tf_op jit(solution)/shard_map/all_to_all | solution.py:249
  17.6 0.0 copy-done
  17.6 0.0 copy-start.1
  17.6 1.0 pad_maximum_fusion.4
  18.6 1.3 collective-permute-start.5
  19.9 4.6 %collective-permute-start.4 = (f32[2,8,2048]{2,1,0:T(8,128)S(1)}, f32[2,8,2048]{2,1,0:T(8,128)S(1)}, u32[]{:S(2)}, u32[]{:S(2)}) collective-permute-start(f32[2,8,2048]{2,1,0:T(8,128)S(1)} %get-tuple-element.9), channel_id=1, source_target_pairs={{0,8},{8,16},{16,24},{1,9},{9,17},{17,25},{2,10},{10,18},{18,26},{... | collective-permute-start | bytes 393224 | tf_op jit(solution)/shard_map/ppermute | solution.py:215
  24.5 23.3 %collective-permute-done.5.eb = f32[2,8,2048]{2,1,0:T(8,128)S(1)} collective-permute-done((f32[2,8,2048]{2,1,0:T(8,128)S(1)}, f32[2,8,2048]{2,1,0:T(8,128)S(1)}, u32[]{:S(2)}, u32[]{:S(2)}) %collective-permute-start.5) | collective-permute-done | bytes 131104 | tf_op jit(solution)/shard_map/ppermute | solution.py:215
  47.8 0.0 copy-start.6
  47.8 8.6 %collective-permute-done.4.et = f32[2,8,2048]{2,1,0:T(8,128)S(1)} collective-permute-done((f32[2,8,2048]{2,1,0:T(8,128)S(1)}, f32[2,8,2048]{2,1,0:T(8,128)S(1)}, u32[]{:S(2)}, u32[]{:S(2)}) %collective-permute-start.4) | collective-permute-done | bytes 131104 | tf_op jit(solution)/shard_map/ppermute | solution.py:215
  56.4 0.0 copy-start.7
  56.4 0.0 copy-done.1
  56.4 0.1 fusion.1
  56.4 0.0 copy-done.6
  56.4 0.6 copy-done.7
  57.0 1.3 collective-permute-start.7
  58.3 3.0 %collective-permute-start.6 = (f32[2,272,128]{2,1,0:T(8,128)S(1)}, f32[2,272,128]{2,1,0:T(8,128)S(1)}, u32[]{:S(2)}, u32[]{:S(2)}) collective-permute-start(f32[2,272,128]{2,1,0:T(8,128)S(1)} %get-tuple-element.7), channel_id=1, source_target_pairs={{0,1},{1,2},{2,3},{3,4},{4,5},{5,6},{6,7},{8,9},{9,10},{10,11},{11... | collective-permute-start | bytes 835592 | tf_op jit(solution)/shard_map/ppermute | solution.py:215
  61.4 7.0 %all-to-all-done.got_ref = f32[32,33,4,128]{3,2,1,0:T(4,128)} async-done(((f32[32,33,4,128]{3,2,1,0:T(4,128)}), f32[32,33,4,128]{3,2,1,0:T(4,128)}, u32[]{:S(2)}, u32[]{:S(2)}) %all-to-all-start) | async-done | bytes 2162720 | tf_op jit(solution)/shard_map/all_to_all | solution.py:249
  68.4 1.5 slice_convert_fusion
  69.8 10.6 %scatter.1.f_in = f32[2,256,2048]{2,1,0:T(8,128)} custom-call(s32[4096]{0:T(1024)} %bitcast.19, f32[32,33,4,128]{3,2,1,0:T(4,128)} %all-to-all-done.got_ref), custom_call_target="tpu_custom_call" | custom-call | tf_op jit(solution)/shard_map/scatter/pallas_call | solution.py:252
  80.4 1.0 fusion.5
  81.4 1.3 collective-permute-start.1
  82.7 11.6 %collective-permute-start = (f32[2,8,2048]{2,1,0:T(8,128)S(1)}, f32[2,8,2048]{2,1,0:T(8,128)S(1)}, u32[]{:S(2)}, u32[]{:S(2)}) collective-permute-start(f32[2,8,2048]{2,1,0:T(8,128)S(1)} %get-tuple-element.13), channel_id=1, source_target_pairs={{0,8},{8,16},{16,24},{1,9},{9,17},{17,25},{2,10},{10,18},{18,26},{... | collective-permute-start | bytes 393224 | tf_op jit(solution)/shard_map/ppermute | solution.py:215
  94.3 1.1 fusion.4
  95.3 1.3 collective-permute-done.1.fb
  96.7 0.0 copy-start.8
  96.7 1.2 collective-permute-done.ft
  97.9 0.0 copy-start.9
  97.9 1.8 %collective-permute-start.2 = (f32[2,272,128]{2,1,0:T(8,128)S(1)}, f32[2,272,128]{2,1,0:T(8,128)S(1)}, u32[]{:S(2)}, u32[]{:S(2)}) collective-permute-start(f32[2,272,128]{2,1,0:T(8,128)S(1)} %pad_maximum_fusion.2), channel_id=1, source_target_pairs={{0,1},{1,2},{2,3},{3,4},{4,5},{5,6},{6,7},{8,9},{9,10},{10,11},{11... | collective-permute-start | bytes 835592 | tf_op jit(solution)/shard_map/ppermute | solution.py:215
  99.7 1.3 collective-permute-start.3
  101.0 0.0 collective-permute-done.7.er
  101.0 0.0 copy-start.2
  101.0 0.0 collective-permute-done.6.el
  101.0 0.0 copy-start.3
  101.0 0.0 collective-permute-done.2.fl
  101.0 0.0 copy-start.4
  101.1 13.3 %collective-permute-done.3.fr = f32[2,272,128]{2,1,0:T(8,128)S(1)} collective-permute-done((f32[2,272,128]{2,1,0:T(8,128)S(1)}, f32[2,272,128]{2,1,0:T(8,128)S(1)}, u32[]{:S(2)}, u32[]{:S(2)}) %collective-permute-start.3) | collective-permute-done | bytes 278560 | tf_op jit(solution)/shard_map/ppermute | solution.py:215
  114.3 0.0 copy-done.8
  114.3 0.0 copy-done.9
  114.3 0.0 copy-done.2
  114.3 0.0 copy-done.3
  114.3 0.0 copy-done.4
  114.4 0.0 copy-start.5
  114.4 0.7 copy-done.5
  115.1 29.1 %stencil.1 = (f32[2,256,2048]{2,1,0:T(8,128)}, f32[8,2,128]{2,1,0:T(2,128)}) custom-call(f32[2,256,2048]{2,1,0:T(8,128)} %scatter.1.f_in, f32[2,8,2048]{2,1,0:T(8,128)} %copy-done.9, f32[2,8,2048]{2,1,0:T(8,128)} %copy-done.8, f32[2,272,128]{2,1,0:T(8,128)} %copy-done.4, f32[2,272,128]{2,1,0:T(8,128)} %copy-done.5, f32[256,2048]{1,0:T(8,128)} %eta_in.1, ...), custom_call_target="tpu_custom_call" | custom-call | tf_op jit(solution)/shard_map/stencil/pallas_call | solution.py:263
  144.2 16.3 %all_to_all.20 = f32[8,2,128]{2,1,0:T(2,128)S(1)} all-to-all(f32[8,2,128]{2,1,0:T(2,128)} %get-tuple-element.5), channel_id=1, replica_groups=mesh['ty'=4,'tx'=8] {'tx'}, dimensions={0} | all-to-all | bytes 16384 | tf_op jit(solution)/shard_map/all_to_all | solution.py:285
  160.5 0.6 copy.10
  (6 shorter events, 0.1 us)
Async XLA Ops:
  10.2 7.4 %copy-start = (f32[256,2048]{1,0:T(8,128)S(1)}, f32[256,2048]{1,0:T(8,128)}, u32[]{:S(2)}) copy-start(f32[256,2048]{1,0:T(8,128)} %eta_in.1) | copy-start | bytes 6291460
  10.2 58.2 %all-to-all-start = ((f32[32,33,4,128]{3,2,1,0:T(4,128)}), f32[32,33,4,128]{3,2,1,0:T(4,128)}, u32[]{:S(2)}, u32[]{:S(2)}) async-start(f32[32,33,4,128]{3,2,1,0:T(4,128)} %pack.1), calls=%async_computation | async-start | bytes 4325376 | tf_op jit(solution)/shard_map/all_to_all | solution.py:249
  17.6 38.8 %copy-start.1 = (f32[256,2048]{1,0:T(8,128)S(1)}, f32[256,2048]{1,0:T(8,128)}, u32[]{:S(2)}) copy-start(f32[256,2048]{1,0:T(8,128)} %q_in.1) | copy-start | bytes 6291460
  18.6 29.1 %collective-permute-start.5 = (f32[2,8,2048]{2,1,0:T(8,128)S(1)}, f32[2,8,2048]{2,1,0:T(8,128)S(1)}, u32[]{:S(2)}, u32[]{:S(2)}) collective-permute-start(f32[2,8,2048]{2,1,0:T(8,128)S(1)} %get-tuple-element.8), channel_id=1, source_target_pairs={{8,0},{16,8},{24,16},{9,1},{17,9},{25,17},{10,2},{18,10},{26,18},{... | collective-permute-start | bytes 393224 | tf_op jit(solution)/shard_map/ppermute | solution.py:215
  19.9 36.4 %collective-permute-start.4 = (f32[2,8,2048]{2,1,0:T(8,128)S(1)}, f32[2,8,2048]{2,1,0:T(8,128)S(1)}, u32[]{:S(2)}, u32[]{:S(2)}) collective-permute-start(f32[2,8,2048]{2,1,0:T(8,128)S(1)} %get-tuple-element.9), channel_id=1, source_target_pairs={{0,8},{8,16},{16,24},{1,9},{9,17},{17,25},{2,10},{10,18},{18,26},{... | collective-permute-start | bytes 393224 | tf_op jit(solution)/shard_map/ppermute | solution.py:215
  47.8 8.7 %copy-start.6 = (f32[2,8,2048]{2,1,0:T(8,128)}, f32[2,8,2048]{2,1,0:T(8,128)S(1)}, u32[]{:S(2)}) copy-start(f32[2,8,2048]{2,1,0:T(8,128)S(1)} %collective-permute-done.5.eb) | copy-start | bytes 393220
  56.4 0.7 copy-start.7
  57.0 44.0 %collective-permute-start.7 = (f32[2,272,128]{2,1,0:T(8,128)S(1)}, f32[2,272,128]{2,1,0:T(8,128)S(1)}, u32[]{:S(2)}, u32[]{:S(2)}) collective-permute-start(f32[2,272,128]{2,1,0:T(8,128)S(1)} %get-tuple-element.6), channel_id=1, source_target_pairs={{1,0},{2,1},{3,2},{4,3},{5,4},{6,5},{7,6},{9,8},{10,9},{11,10},{12... | collective-permute-start | bytes 835592 | tf_op jit(solution)/shard_map/ppermute | solution.py:215
  58.3 42.7 %collective-permute-start.6 = (f32[2,272,128]{2,1,0:T(8,128)S(1)}, f32[2,272,128]{2,1,0:T(8,128)S(1)}, u32[]{:S(2)}, u32[]{:S(2)}) collective-permute-start(f32[2,272,128]{2,1,0:T(8,128)S(1)} %get-tuple-element.7), channel_id=1, source_target_pairs={{0,1},{1,2},{2,3},{3,4},{4,5},{5,6},{6,7},{8,9},{9,10},{10,11},{11... | collective-permute-start | bytes 835592 | tf_op jit(solution)/shard_map/ppermute | solution.py:215
  81.4 15.3 %collective-permute-start.1 = (f32[2,8,2048]{2,1,0:T(8,128)S(1)}, f32[2,8,2048]{2,1,0:T(8,128)S(1)}, u32[]{:S(2)}, u32[]{:S(2)}) collective-permute-start(f32[2,8,2048]{2,1,0:T(8,128)S(1)} %get-tuple-element.12), channel_id=1, source_target_pairs={{8,0},{16,8},{24,16},{9,1},{17,9},{25,17},{10,2},{18,10},{26,18},{... | collective-permute-start | bytes 393224 | tf_op jit(solution)/shard_map/ppermute | solution.py:215
  82.7 15.2 %collective-permute-start = (f32[2,8,2048]{2,1,0:T(8,128)S(1)}, f32[2,8,2048]{2,1,0:T(8,128)S(1)}, u32[]{:S(2)}, u32[]{:S(2)}) collective-permute-start(f32[2,8,2048]{2,1,0:T(8,128)S(1)} %get-tuple-element.13), channel_id=1, source_target_pairs={{0,8},{8,16},{16,24},{1,9},{9,17},{17,25},{2,10},{10,18},{18,26},{... | collective-permute-start | bytes 393224 | tf_op jit(solution)/shard_map/ppermute | solution.py:215
  96.7 17.7 %copy-start.8 = (f32[2,8,2048]{2,1,0:T(8,128)}, f32[2,8,2048]{2,1,0:T(8,128)S(1)}, u32[]{:S(2)}) copy-start(f32[2,8,2048]{2,1,0:T(8,128)S(1)} %collective-permute-done.1.fb) | copy-start | bytes 393220
  97.9 16.5 %copy-start.9 = (f32[2,8,2048]{2,1,0:T(8,128)}, f32[2,8,2048]{2,1,0:T(8,128)S(1)}, u32[]{:S(2)}) copy-start(f32[2,8,2048]{2,1,0:T(8,128)S(1)} %collective-permute-done.ft) | copy-start | bytes 393220
  97.9 3.1 %collective-permute-start.2 = (f32[2,272,128]{2,1,0:T(8,128)S(1)}, f32[2,272,128]{2,1,0:T(8,128)S(1)}, u32[]{:S(2)}, u32[]{:S(2)}) collective-permute-start(f32[2,272,128]{2,1,0:T(8,128)S(1)} %pad_maximum_fusion.2), channel_id=1, source_target_pairs={{0,1},{1,2},{2,3},{3,4},{4,5},{5,6},{6,7},{8,9},{9,10},{10,11},{11... | collective-permute-start | bytes 835592 | tf_op jit(solution)/shard_map/ppermute | solution.py:215
  99.7 14.6 %collective-permute-start.3 = (f32[2,272,128]{2,1,0:T(8,128)S(1)}, f32[2,272,128]{2,1,0:T(8,128)S(1)}, u32[]{:S(2)}, u32[]{:S(2)}) collective-permute-start(f32[2,272,128]{2,1,0:T(8,128)S(1)} %pad_maximum_fusion.3), channel_id=1, source_target_pairs={{1,0},{2,1},{3,2},{4,3},{5,4},{6,5},{7,6},{9,8},{10,9},{11,10},{12... | collective-permute-start | bytes 835592 | tf_op jit(solution)/shard_map/ppermute | solution.py:215
  101.0 13.3 %copy-start.2 = (f32[2,272,128]{2,1,0:T(8,128)}, f32[2,272,128]{2,1,0:T(8,128)S(1)}, u32[]{:S(2)}) copy-start(f32[2,272,128]{2,1,0:T(8,128)S(1)} %collective-permute-done.7.er) | copy-start | bytes 835588
  101.0 13.3 %copy-start.3 = (f32[2,272,128]{2,1,0:T(8,128)}, f32[2,272,128]{2,1,0:T(8,128)S(1)}, u32[]{:S(2)}) copy-start(f32[2,272,128]{2,1,0:T(8,128)S(1)} %collective-permute-done.6.el) | copy-start | bytes 835588
  101.0 13.3 %copy-start.4 = (f32[2,272,128]{2,1,0:T(8,128)}, f32[2,272,128]{2,1,0:T(8,128)S(1)}, u32[]{:S(2)}) copy-start(f32[2,272,128]{2,1,0:T(8,128)S(1)} %collective-permute-done.2.fl) | copy-start | bytes 835588
  114.4 0.7 copy-start.5

commit v2 on v1

--- a/solution.py
+++ b/solution.py
@@ -65,7 +65,7 @@
 
 
 def stencil_kernel(
-    f_in, ft, fb, fl, fr, eta_in, q_in, et, eb, el, er, vel_in,
+    f_in, ft, fb, fl, fr, eta_in, q_in, et, eb, el, er, qt, qb, ql, qr, vel_in,
     adj_out, coarse_out,
     f, eta, q, a0, a1, inv, vel, gsum, sems,
 ):
@@ -78,11 +78,9 @@
     left = (pl.ds(R0 - RH, rows + 2 * RH), pl.ds(0, CH))
     right = (pl.ds(R0 - RH, rows + 2 * RH), pl.ds(CH + cols, CH))
     moves = []
-    for i, (core, field) in enumerate(((eta_in, eta), (q_in, q))):
-        moves.append((core, field.at[mid]))
-        for edge, spot in ((et, top), (eb, bottom), (el, left), (er, right)):
-            moves.append((edge.at[i], field.at[spot]))
-    n_first = len(moves)
+    for field, *parts in ((eta, eta_in, et, eb, el, er), (q, q_in, qt, qb, ql, qr)):
+        for part, spot in zip(parts, (mid, top, bottom, left, right)):
+            moves.append((part, field.at[spot]))
     for c in range(2):
         moves.append((f_in.at[c], f.at[(c,) + mid]))
         for edge, spot in ((ft, top), (fb, bottom), (fl, left), (fr, right)):
@@ -206,21 +204,176 @@
         coarse_out[i] = coarse[i * share : (i + 1) * share]
 
 
-def halos(x):
-    rows, cols = x.shape[1:]
-
-    def both(axis, last, first):
-        up = [(i, i + 1) for i in range(lax.axis_size(axis) - 1)]
-        down = [(j, i) for i, j in up]
-        return lax.ppermute(last, axis, up), lax.ppermute(first, axis, down)
-
-    top, bottom = both("ty", x[:, rows - RH :], x[:, :RH])
-
-    def side(part):
-        return jnp.concatenate([top[:, :, part], x[:, :, part], bottom[:, :, part]], axis=1)
-
-    left, right = both("tx", side(slice(cols - CH, cols)), side(slice(0, CH)))
-    return top, bottom, left, right
+SIDES = [(dy, dx) for dy in (-1, 0, 1) for dx in (-1, 0, 1) if (dy, dx) != (0, 0)]
+
+
+def present(dy, dx):
+    y, x = lax.axis_index("ty") + dy, lax.axis_index("tx") + dx
+    inside = (y >= 0) & (y < lax.axis_size("ty")) & (x >= 0) & (x < lax.axis_size("tx"))
+    return inside, (y, x)
+
+
+def edge_spots(dy, dx, core, halo):
+    top, bottom, left, right = halo
+    rows, cols = core.shape[-2:]
+    lead = (slice(None),) * (len(core.shape) - 2)
+    y = {-1: pl.ds(0, RH), 0: pl.ds(0, rows), 1: pl.ds(rows - RH, RH)}[dy]
+    x = {-1: pl.ds(0, CH), 0: pl.ds(0, cols), 1: pl.ds(cols - CH, CH)}[dx]
+    if dx == 0:
+        target = top if dy == 1 else bottom
+    else:
+        strip = left if dx == 1 else right
+        span = {1: pl.ds(0, RH), 0: pl.ds(RH, rows), -1: pl.ds(RH + rows, RH)}[dy]
+        target = strip.at[lead + (span, slice(None))]
+    return core.at[lead + (y, x)], target
+
+
+def edge_copies(fields, send, recv):
+    for i, (dy, dx) in enumerate(SIDES):
+        for j, (core, halo) in enumerate(fields):
+            src, dst = edge_spots(dy, dx, core, halo)
+            there, where = present(dy, dx)
+            k = i * len(fields) + j
+            copy = pltpu.make_async_remote_copy(
+                src_ref=src,
+                dst_ref=dst,
+                send_sem=send.at[k],
+                recv_sem=recv.at[k],
+                device_id=where,
+                device_id_type=pl.DeviceIdType.MESH,
+            )
+            yield copy, dst, there, present(-dy, -dx)[0]
+
+
+def start_edges(fields, send, recv):
+    for copy, dst, there, source in edge_copies(fields, send, recv):
+
+        @pl.when(there)
+        def _(copy=copy):
+            copy.start()
+
+        @pl.when(jnp.logical_not(source))
+        def _(dst=dst):
+            dst[...] = jnp.zeros(dst.shape, jnp.float32)
+
+
+def finish_edges(fields, send, recv):
+    for copy, _, there, source in edge_copies(fields, send, recv):
+
+        @pl.when(there)
+        def _(copy=copy):
+            copy.wait_send()
+
+        @pl.when(source)
+        def _(copy=copy):
+            copy.wait_recv()
+
+
+def exchange_kernel(
+    packed, eta, q, got, et, eb, el, er, qt, qb, ql, qr,
+    send, recv, edge_send, edge_recv, local,
+):
+    devices = packed.shape[0]
+    ntx = lax.axis_size("tx")
+    me = lax.axis_index("ty") * ntx + lax.axis_index("tx")
+    barrier = pltpu.get_barrier_semaphore()
+
+    def place(d):
+        target = lax.rem(me + d, devices)
+        return target, (target // ntx, lax.rem(target, ntx))
+
+    def greet(d, carry):
+        pl.semaphore_signal(
+            barrier, inc=1, device_id=place(d)[1], device_id_type=pl.DeviceIdType.MESH
+        )
+        return carry
+
+    lax.fori_loop(1, devices, greet, 0)
+    pl.semaphore_wait(barrier, devices - 1)
+
+    def row_copy(d):
+        target, where = place(d)
+        return pltpu.make_async_remote_copy(
+            src_ref=packed.at[target],
+            dst_ref=got.at[me],
+            send_sem=send.at[d],
+            recv_sem=recv.at[d],
+            device_id=where,
+            device_id_type=pl.DeviceIdType.MESH,
+        )
+
+    def begin(d, carry):
+        row_copy(d).start()
+        return carry
+
+    lax.fori_loop(1, devices, begin, 0)
+    own = pltpu.make_async_copy(packed.at[me], got.at[me], local)
+    own.start()
+    fields = [(eta, (et, eb, el, er)), (q, (qt, qb, ql, qr))]
+    start_edges(fields, edge_send, edge_recv)
+    finish_edges(fields, edge_send, edge_recv)
+    own.wait()
+
+    def finish(d, carry):
+        copy = row_copy(d)
+        copy.wait_send()
+        copy.wait_recv()
+        return carry
+
+    lax.fori_loop(1, devices, finish, 0)
+
+
+def edge_kernel(f, ft, fb, fl, fr, send, recv):
+    barrier = pltpu.get_barrier_semaphore()
+    for dy, dx in SIDES:
+        there, where = present(dy, dx)
+
+        @pl.when(there)
+        def _(where=where):
+            pl.semaphore_signal(
+                barrier, inc=1, device_id=where, device_id_type=pl.DeviceIdType.MESH
+            )
+
+    peers = sum(present(dy, dx)[0].astype(jnp.int32) for dy, dx in SIDES)
+    pl.semaphore_wait(barrier, peers)
+
+    fields = [(f, (ft, fb, fl, fr))]
+    start_edges(fields, send, recv)
+    finish_edges(fields, send, recv)
+
+
+def coarse_kernel(part, out, held, send, recv):
+    count = part.shape[0]
+    ty, me = lax.axis_index("ty"), lax.axis_index("tx")
+    barrier = pltpu.get_barrier_semaphore()
+    for d in range(1, count):
+        pl.semaphore_signal(
+            barrier,
+            inc=1,
+            device_id=(ty, lax.rem(me + d, count)),
+            device_id_type=pl.DeviceIdType.MESH,
+        )
+    pl.semaphore_wait(barrier, count - 1)
+    copies = []
+    for d in range(1, count):
+        target = lax.rem(me + d, count)
+        copy = pltpu.make_async_remote_copy(
+            src_ref=part.at[target],
+            dst_ref=held.at[me],
+            send_sem=send.at[d],
+            recv_sem=recv.at[d],
+            device_id=(ty, target),
+            device_id_type=pl.DeviceIdType.MESH,
+        )
+        copy.start()
+        copies.append(copy)
+    held[me] = part[me]
+    for copy in copies:
+        copy.wait_send()
+        copy.wait_recv()
+    width = part.shape[2]
+    for i in range(count):
+        out[:, i * width : (i + 1) * width] = held[i]
 
 
 VMEM = pl.BlockSpec(memory_space=pltpu.VMEM)
@@ -246,8 +399,29 @@
         compiler_params=params,
         name="pack",
     )(track_tile[:, 0], track_slot, block)
-    got = lax.all_to_all(packed, ("ty", "tx"), split_axis=0, concat_axis=0, tiled=True)
-    eq_halo = halos(jnp.stack([viscosity, log_friction]))
+    halo = [(RH, cols), (RH, cols), (rows + 2 * RH, CH), (rows + 2 * RH, CH)]
+
+    def remote(number):
+        return pltpu.CompilerParams(
+            collective_id=number, has_side_effects=True, vmem_limit_bytes=VMEM_LIMIT
+        )
+
+    got, *eq_halo = pl.pallas_call(
+        exchange_kernel,
+        out_shape=[jax.ShapeDtypeStruct(packed.shape, f32)]
+        + [jax.ShapeDtypeStruct(shape, f32) for shape in halo * 2],
+        in_specs=[ANY] * 3,
+        out_specs=[ANY] + [VMEM] * 8,
+        scratch_shapes=[
+            pltpu.SemaphoreType.DMA((devices,)),
+            pltpu.SemaphoreType.DMA((devices,)),
+            pltpu.SemaphoreType.DMA((16,)),
+            pltpu.SemaphoreType.DMA((16,)),
+            pltpu.SemaphoreType.DMA,
+        ],
+        compiler_params=remote(0),
+        name="exchange",
+    )(packed, viscosity, log_friction)
     meta = got[:, cap, 0, :].astype(jnp.int32).reshape(devices * 128)
     forcing = pl.pallas_call(
         functools.partial(scatter_kernel, cap, cols // seg),
@@ -257,7 +431,15 @@
         compiler_params=params,
         name="scatter",
     )(meta, got)
-    f_halo = halos(forcing)
+    f_halo = pl.pallas_call(
+        edge_kernel,
+        out_shape=[jax.ShapeDtypeStruct((2,) + shape, f32) for shape in halo],
+        in_specs=[ANY],
+        out_specs=[VMEM] * 4,
+        scratch_shapes=[pltpu.SemaphoreType.DMA((8,)), pltpu.SemaphoreType.DMA((8,))],
+        compiler_params=remote(1),
+        name="edges",
+    )(forcing)
     coarse_rows = rows // CB
     big = (rows + 2 * R0, cols + 2 * CH)
     adjoint, coarse = pl.pallas_call(
@@ -266,7 +448,7 @@
             jax.ShapeDtypeStruct((2, rows, cols), f32),
             jax.ShapeDtypeStruct((tiles_x, coarse_rows // tiles_x, cols // CB), f32),
         ),
-        in_specs=[ANY] * 12,
+        in_specs=[ANY] * 16,
         out_specs=(VMEM, VMEM),
         scratch_shapes=[
             pltpu.VMEM((2,) + big, f32),
@@ -282,8 +464,20 @@
         compiler_params=params,
         name="stencil",
     )(forcing, *f_halo, viscosity, log_friction, *eq_halo, velocity)
-    grad = lax.all_to_all(coarse, "tx", split_axis=0, concat_axis=2, tiled=True)
-    return adjoint, grad[0]
+    grad = pl.pallas_call(
+        coarse_kernel,
+        out_shape=jax.ShapeDtypeStruct((coarse_rows // tiles_x, cols // CB * tiles_x), f32),
+        in_specs=[VMEM],
+        out_specs=VMEM,
+        scratch_shapes=[
+            pltpu.VMEM(coarse.shape, f32),
+            pltpu.SemaphoreType.DMA((tiles_x,)),
+            pltpu.SemaphoreType.DMA((tiles_x,)),
+        ],
+        compiler_params=remote(2),
+        name="coarse",
+    )(coarse)
+    return adjoint, grad
 
 
 def solution(mesh):

time: 161 us -> 148 us (0.919)
  Pallas kernels: 49.2 us -> 144 us
  waiting for transfers between devices: 54.6 us -> 0 us
  starting transfers between devices: 33.5 us -> 0 us
  blocking collectives: 16.3 us -> 0 us
  local copies, waits for them, and re-layouts: 4 us -> 1.3 us
    pallas_call x0 -> x3, Pallas kernels: none -> 82.4 us  [the longest x1 50.5 us: shards(): pl.pallas_call(exchange_kernel, out_shape=[jax.ShapeDtypeStruct(packed.sh...]
    ppermute x8 -> x0, waiting for transfers between devices: 47.6 us -> none  [both(): return (lax.ppermute(last, axis, up), lax.ppermute(first, axis, down))]
    ppermute x8 -> x0, starting transfers between devices: 26.1 us -> none  [both(): return (lax.ppermute(last, axis, up), lax.ppermute(first, axis, down))]
    all_to_all x1 -> x0, blocking collectives: 16.3 us -> none  [shards(): grad = lax.all_to_all(coarse, 'tx', split_axis=0, concat_axis=2, tiled=True)]
    pallas_call x1, Pallas kernels: 10.6 us -> 23.2 us  [shards(): pl.pallas_call(functools.partial(scatter_kernel, cap, cols // seg), out_s...]
    all_to_all x1 -> x0, starting transfers between devices: 7.41 us -> none  [shards(): lax.all_to_all(packed, ('ty', 'tx'), split_axis=0, concat_axis=0, tiled=T...]
    all_to_all x1 -> x0, waiting for transfers between devices: 6.98 us -> none  [shards(): lax.all_to_all(packed, ('ty', 'tx'), split_axis=0, concat_axis=0, tiled=T...]
    slice x6 -> x0, local copies, waits for them, and re-layouts: 2.06 us -> none  [the longest x1 1.07 us: side(): x[:, :, part]]
  transfers between devices with their start and end apart: 9 -> 0, of which waited for: 6 -> 0; matrix products, arithmetic and copies ran while one was open for 3% -> 0% of each run, Pallas kernels for 7% -> 0%
where the time goes in v2:
time: 148 us
  Pallas kernels  144 us (97%)
    pallas_call x1, Pallas kernels, shards(): pl.pallas_call(exchange_kernel, out_shape=[jax.ShapeDtypeStruct(packed.sh...  50.5 us
    pallas_call x1, Pallas kernels, shards(): pl.pallas_call(stencil_kernel, out_shape=(jax.ShapeDtypeStruct((2, rows,...  29.1 us
    pallas_call x1, Pallas kernels, shards(): pl.pallas_call(functools.partial(scatter_kernel, cap, cols // seg), out_s...  23.2 us
    pallas_call x1, Pallas kernels, shards(): pl.pallas_call(edge_kernel, out_shape=[jax.ShapeDtypeStruct((2,) + shape,...  20.6 us
    pallas_call x1, Pallas kernels, shards(): pl.pallas_call(coarse_kernel, out_shape=jax.ShapeDtypeStruct((coarse_rows...  11.2 us
    pallas_call x1, Pallas kernels, shards(): pl.pallas_call(functools.partial(pack_kernel, cap), out_shape=jax.ShapeDt...  9.53 us

profile of v2, /device:TPU:0, one launch (start us, length us, event | category | flops | bytes accessed | tf_op | source)
XLA Modules:
  0.0 147.6 jit_solution(9583673426641775667)
XLA Ops:
  0.6 9.5 %pack.1.packed = f32[32,33,4,128]{3,2,1,0:T(4,128)} custom-call(s32[512]{0:T(512)} %bitcast.9, s32[512]{0:T(512)} %slot_ref.1, f32[512,4,128]{2,1,0:T(4,128)} %bitcast.7), custom_call_target="tpu_custom_call" | custom-call | tf_op jit(solution)/shard_map/pack/pallas_call | solution.py:393
  10.2 50.5 %exchange.1 = (f32[32,33,4,128]{3,2,1,0:T(4,128)}, f32[8,2048]{1,0:T(8,128)}, f32[8,2048]{1,0:T(8,128)}, f32[272,128]{1,0:T(8,128)}, f32[272,128]{1,0:T(8,128)},...) custom-call(f32[32,33,4,128]{3,2,1,0:T(4,128)} %pack.1.packed, ...), custom_call_target="tpu_custom_call" | custom-call | tf_op jit(solution)/shard_map/exchange/pallas_call | solution.py:409
  60.7 1.5 slice_convert_fusion
  62.2 23.2 %scatter.1.f.f_in = f32[2,256,2048]{2,1,0:T(8,128)} custom-call(s32[4096]{0:T(1024)} %bitcast.8, f32[32,33,4,128]{3,2,1,0:T(4,128)} %get-tuple-element.17.got_ref), custom_call_target="tpu_custom_call" | custom-call | tf_op jit(solution)/shard_map/scatter/pallas_call | solution.py:426
  85.3 20.6 %edges.1 = (f32[2,8,2048]{2,1,0:T(8,128)}, f32[2,8,2048]{2,1,0:T(8,128)}, f32[2,272,128]{2,1,0:T(8,128)}, f32[2,272,128]{2,1,0:T(8,128)}) custom-call(f32[2,256,2048]{2,1,0:T(8,128)} %scatter.1.f.f_in), custom_call_target="tpu_custom_call" | custom-call | tf_op jit(solution)/shard_map/edges/pallas_call | solution.py:434
  105.9 29.1 %stencil.1 = (f32[2,256,2048]{2,1,0:T(8,128)}, f32[8,2,128]{2,1,0:T(2,128)}) custom-call(f32[2,256,2048]{2,1,0:T(8,128)} %scatter.1.f.f_in, f32[2,8,2048]{2,1,0:T(8,128)} %get-tuple-element.18.ft, f32[2,8,2048]{2,1,0:T(8,128)} %get-tuple-element.19.fb, f32[2,272,128]{2,1,0:T(8,128)} %get-tuple-element.20.fl, f32[2,272,128]{2,1,0:T(8,128)} %get-tuple-element.21.fr, ...), custom_call_target="tpu_custom_call" | custom-call | tf_op jit(solution)/shard_map/stencil/pallas_call | solution.py:445
  135.1 11.2 %coarse.1 = f32[2,1024]{1,0:T(2,128)} custom-call(f32[8,2,128]{2,1,0:T(2,128)} %get-tuple-element.31.part), custom_call_target="tpu_custom_call" | custom-call | tf_op jit(solution)/shard_map/coarse/pallas_call | solution.py:467
  146.3 1.3 copy.10

commit v3 on v2

--- a/solution.py
+++ b/solution.py
@@ -16,8 +16,34 @@
 VMEM_LIMIT = 56 * 1024 * 1024
 
 
-def pack_kernel(cap, tile_ref, slot_ref, rows_ref, out_ref, count):
+def compact(fields):
+    half = RH // 2
+    north = [top[:half] for top, _, _, _ in fields]
+    south = [bottom[half:] for _, bottom, _, _ in fields]
+    west = [left.T[:half] for _, _, left, _ in fields]
+    east = [right.T[CH - half :] for _, _, _, right in fields]
+    return [jnp.concatenate(parts, axis=0) for parts in (north, south, west, east)]
+
+
+def pack_kernel(
+    cap, tile_ref, slot_ref, rows_ref, eta_in, q_in,
+    out_ref, north, south, west, east,
+    count, row_edges, col_edges, sems,
+):
     devices = out_ref.shape[0]
+    rows, cols = eta_in.shape
+    copies = []
+    for i, x in enumerate((eta_in, q_in)):
+        spots = (
+            (x.at[pl.ds(0, RH), :], row_edges.at[2 * i]),
+            (x.at[pl.ds(rows - RH, RH), :], row_edges.at[2 * i + 1]),
+            (x.at[:, pl.ds(0, CH)], col_edges.at[2 * i]),
+            (x.at[:, pl.ds(cols - CH, CH)], col_edges.at[2 * i + 1]),
+        )
+        for j, (src, dst) in enumerate(spots):
+            copies.append(pltpu.make_async_copy(src, dst, sems.at[4 * i + j]))
+    for copy in copies:
+        copy.start()
     lanes = lax.broadcasted_iota(jnp.int32, (4, 128), 1)
 
     def clear(d, carry):
@@ -39,9 +65,17 @@
         return carry
 
     lax.fori_loop(0, rows_ref.shape[0], place, 0)
-
-
-def scatter_kernel(cap, segs, meta_ref, got_ref, out_ref):
+    for copy in copies:
+        copy.wait()
+    fields = [
+        (row_edges[2 * i], row_edges[2 * i + 1], col_edges[2 * i], col_edges[2 * i + 1])
+        for i in range(2)
+    ]
+    for ref, value in zip((north, south, west, east), compact(fields)):
+        ref[...] = value
+
+
+def scatter_kernel(cap, segs, meta_ref, got_ref, out_ref, north, south, west, east):
     out_ref[...] = jnp.zeros_like(out_ref)
     lanes = lax.broadcasted_iota(jnp.int32, (8, 128), 0)
 
@@ -62,10 +96,22 @@
         return lax.fori_loop(0, meta_ref[s * 128 + cap], add, carry)
 
     lax.fori_loop(0, got_ref.shape[0], source, 0)
+    _, rows, cols = out_ref.shape
+    fields = [
+        (
+            out_ref[c, :RH, :],
+            out_ref[c, rows - RH :, :],
+            out_ref[c, :, :CH],
+            out_ref[c, :, cols - CH :],
+        )
+        for c in range(2)
+    ]
+    for ref, value in zip((north, south, west, east), compact(fields)):
+        ref[...] = value
 
 
 def stencil_kernel(
-    f_in, ft, fb, fl, fr, eta_in, q_in, et, eb, el, er, qt, qb, ql, qr, vel_in,
+    f_in, ft, fb, fl, fr, fc, eta_in, q_in, et, eb, el, er, ec, vel_in,
     adj_out, coarse_out,
     f, eta, q, a0, a1, inv, vel, gsum, sems,
 ):
@@ -73,23 +119,46 @@
     width = cols + 2 * CH
     ty, tx = lax.axis_index("ty"), lax.axis_index("tx")
     mid = (pl.ds(R0, rows), pl.ds(CH, cols))
-    top = (pl.ds(R0 - RH, RH), pl.ds(CH, cols))
-    bottom = (pl.ds(R0 + rows, RH), pl.ds(CH, cols))
-    left = (pl.ds(R0 - RH, rows + 2 * RH), pl.ds(0, CH))
-    right = (pl.ds(R0 - RH, rows + 2 * RH), pl.ds(CH + cols, CH))
-    moves = []
-    for field, *parts in ((eta, eta_in, et, eb, el, er), (q, q_in, qt, qb, ql, qr)):
-        for part, spot in zip(parts, (mid, top, bottom, left, right)):
-            moves.append((part, field.at[spot]))
+    moves = [(eta_in, eta.at[mid]), (q_in, q.at[mid])]
     for c in range(2):
         moves.append((f_in.at[c], f.at[(c,) + mid]))
-        for edge, spot in ((ft, top), (fb, bottom), (fl, left), (fr, right)):
-            moves.append((edge.at[c], f.at[(c,) + spot]))
     n_second = len(moves)
     moves.append((vel_in, vel))
     copies = [pltpu.make_async_copy(a, b, sems.at[i]) for i, (a, b) in enumerate(moves)]
     for copy in copies:
         copy.start()
+    half = RH // 2
+    above, below = slice(R0 - RH, R0), slice(R0 + rows, R0 + rows + RH)
+    core, first, last = slice(CH, CH + cols), slice(0, CH), slice(CH + cols, width)
+
+    def spread(i, edges, put):
+        top, bottom, left, right, corner = edges
+        own = slice(half * i, half * i + half)
+        for span, x, block in (
+            (above, core, top[own, :]),
+            (below, core, bottom[own, :]),
+            (above, first, corner[0, own, :]),
+            (above, last, corner[1, own, :]),
+            (below, first, corner[2, own, :]),
+            (below, last, corner[3, own, :]),
+        ):
+            rest = jnp.zeros_like(block)
+            parts = [rest, block] if span == above else [block, rest]
+            put(span, x, jnp.concatenate(parts, axis=0))
+        rest = jnp.zeros((CH - half, rows), jnp.float32)
+        tall = slice(R0, R0 + rows)
+        put(tall, first, jnp.concatenate([rest, left[own, :]], axis=0).T)
+        put(tall, last, jnp.concatenate([right[own, :], rest], axis=0).T)
+
+    def put_into(ref, *lead):
+        def put(y, x, value):
+            ref[lead + (y, x)] = value
+
+        return put
+
+    for i in range(2):
+        spread(i, (et, eb, el, er, ec), put_into((eta, q)[i]))
+        spread(i, (ft, fb, fl, fr, fc), put_into(f, i))
     for copy in copies[:n_second]:
         copy.wait()
 
@@ -214,39 +283,35 @@
 
 
 def edge_spots(dy, dx, core, halo):
-    top, bottom, left, right = halo
-    rows, cols = core.shape[-2:]
-    lead = (slice(None),) * (len(core.shape) - 2)
-    y = {-1: pl.ds(0, RH), 0: pl.ds(0, rows), 1: pl.ds(rows - RH, RH)}[dy]
-    x = {-1: pl.ds(0, CH), 0: pl.ds(0, cols), 1: pl.ds(cols - CH, CH)}[dx]
+    north, south, west, east = core
+    top, bottom, left, right, corner = halo
     if dx == 0:
-        target = top if dy == 1 else bottom
-    else:
-        strip = left if dx == 1 else right
-        span = {1: pl.ds(0, RH), 0: pl.ds(RH, rows), -1: pl.ds(RH + rows, RH)}[dy]
-        target = strip.at[lead + (span, slice(None))]
-    return core.at[lead + (y, x)], target
-
-
-def edge_copies(fields, send, recv):
-    for i, (dy, dx) in enumerate(SIDES):
-        for j, (core, halo) in enumerate(fields):
-            src, dst = edge_spots(dy, dx, core, halo)
-            there, where = present(dy, dx)
-            k = i * len(fields) + j
-            copy = pltpu.make_async_remote_copy(
-                src_ref=src,
-                dst_ref=dst,
-                send_sem=send.at[k],
-                recv_sem=recv.at[k],
-                device_id=where,
-                device_id_type=pl.DeviceIdType.MESH,
-            )
-            yield copy, dst, there, present(-dy, -dx)[0]
-
-
-def start_edges(fields, send, recv):
-    for copy, dst, there, source in edge_copies(fields, send, recv):
+        return (north, bottom) if dy == -1 else (south, top)
+    if dy == 0:
+        return (west, right) if dx == -1 else (east, left)
+    src = north if dy == -1 else south
+    start = 0 if dx == -1 else src.shape[1] - CH
+    k = (0 if dy == 1 else 2) + (0 if dx == 1 else 1)
+    return src.at[:, pl.ds(start, CH)], corner.at[k]
+
+
+def edge_copies(core, halo, send, recv):
+    for k, (dy, dx) in enumerate(SIDES):
+        src, dst = edge_spots(dy, dx, core, halo)
+        there, where = present(dy, dx)
+        copy = pltpu.make_async_remote_copy(
+            src_ref=src,
+            dst_ref=dst,
+            send_sem=send.at[k],
+            recv_sem=recv.at[k],
+            device_id=where,
+            device_id_type=pl.DeviceIdType.MESH,
+        )
+        yield copy, dst, there, present(-dy, -dx)[0]
+
+
+def start_edges(core, halo, send, recv):
+    for copy, dst, there, source in edge_copies(core, halo, send, recv):
 
         @pl.when(there)
         def _(copy=copy):
@@ -257,8 +322,8 @@
             dst[...] = jnp.zeros(dst.shape, jnp.float32)
 
 
-def finish_edges(fields, send, recv):
-    for copy, _, there, source in edge_copies(fields, send, recv):
+def finish_edges(core, halo, send, recv):
+    for copy, _, there, source in edge_copies(core, halo, send, recv):
 
         @pl.when(there)
         def _(copy=copy):
@@ -270,7 +335,7 @@
 
 
 def exchange_kernel(
-    packed, eta, q, got, et, eb, el, er, qt, qb, ql, qr,
+    packed, north, south, west, east, got, top, bottom, left, right, corner,
     send, recv, edge_send, edge_recv, local,
 ):
     devices = packed.shape[0]
@@ -309,9 +374,9 @@
     lax.fori_loop(1, devices, begin, 0)
     own = pltpu.make_async_copy(packed.at[me], got.at[me], local)
     own.start()
-    fields = [(eta, (et, eb, el, er)), (q, (qt, qb, ql, qr))]
-    start_edges(fields, edge_send, edge_recv)
-    finish_edges(fields, edge_send, edge_recv)
+    edges = ((north, south, west, east), (top, bottom, left, right, corner))
+    start_edges(*edges, edge_send, edge_recv)
+    finish_edges(*edges, edge_send, edge_recv)
     own.wait()
 
     def finish(d, carry):
@@ -323,7 +388,7 @@
     lax.fori_loop(1, devices, finish, 0)
 
 
-def edge_kernel(f, ft, fb, fl, fr, send, recv):
+def edge_kernel(north, south, west, east, top, bottom, left, right, corner, send, recv):
     barrier = pltpu.get_barrier_semaphore()
     for dy, dx in SIDES:
         there, where = present(dy, dx)
@@ -337,9 +402,9 @@
     peers = sum(present(dy, dx)[0].astype(jnp.int32) for dy, dx in SIDES)
     pl.semaphore_wait(barrier, peers)
 
-    fields = [(f, (ft, fb, fl, fr))]
-    start_edges(fields, send, recv)
-    finish_edges(fields, send, recv)
+    edges = ((north, south, west, east), (top, bottom, left, right, corner))
+    start_edges(*edges, send, recv)
+    finish_edges(*edges, send, recv)
 
 
 def coarse_kernel(part, out, held, send, recv):
@@ -390,16 +455,24 @@
     params = pltpu.CompilerParams(vmem_limit_bytes=VMEM_LIMIT)
     f32 = jnp.float32
     block = track_rows.reshape(rows_dev, 2, 2, 128).transpose(0, 2, 1, 3).reshape(rows_dev, 4, 128)
-    packed = pl.pallas_call(
+    edge_shapes = [
+        jax.ShapeDtypeStruct(shape, f32) for shape in ((RH, cols),) * 2 + ((RH, rows),) * 2
+    ]
+    halo_shapes = edge_shapes + [jax.ShapeDtypeStruct((4, RH, CH), f32)]
+    packed, *eq_edges = pl.pallas_call(
         functools.partial(pack_kernel, cap),
-        out_shape=jax.ShapeDtypeStruct((devices, cap + 1, 4, 128), f32),
-        in_specs=[SMEM, SMEM, VMEM],
-        out_specs=VMEM,
-        scratch_shapes=[pltpu.SMEM((devices,), jnp.int32)],
+        out_shape=[jax.ShapeDtypeStruct((devices, cap + 1, 4, 128), f32)] + edge_shapes,
+        in_specs=[SMEM, SMEM, VMEM, ANY, ANY],
+        out_specs=[VMEM] * 5,
+        scratch_shapes=[
+            pltpu.SMEM((devices,), jnp.int32),
+            pltpu.VMEM((4, RH, cols), f32),
+            pltpu.VMEM((4, rows, CH), f32),
+            pltpu.SemaphoreType.DMA((8,)),
+        ],
         compiler_params=params,
         name="pack",
-    )(track_tile[:, 0], track_slot, block)
-    halo = [(RH, cols), (RH, cols), (rows + 2 * RH, CH), (rows + 2 * RH, CH)]
+    )(track_tile[:, 0], track_slot, block, viscosity, log_friction)
 
     def remote(number):
         return pltpu.CompilerParams(
@@ -408,38 +481,37 @@
 
     got, *eq_halo = pl.pallas_call(
         exchange_kernel,
-        out_shape=[jax.ShapeDtypeStruct(packed.shape, f32)]
-        + [jax.ShapeDtypeStruct(shape, f32) for shape in halo * 2],
-        in_specs=[ANY] * 3,
-        out_specs=[ANY] + [VMEM] * 8,
+        out_shape=[jax.ShapeDtypeStruct(packed.shape, f32)] + halo_shapes,
+        in_specs=[ANY] + [VMEM] * 4,
+        out_specs=[ANY] + [VMEM] * 5,
         scratch_shapes=[
             pltpu.SemaphoreType.DMA((devices,)),
             pltpu.SemaphoreType.DMA((devices,)),
-            pltpu.SemaphoreType.DMA((16,)),
-            pltpu.SemaphoreType.DMA((16,)),
+            pltpu.SemaphoreType.DMA((8,)),
+            pltpu.SemaphoreType.DMA((8,)),
             pltpu.SemaphoreType.DMA,
         ],
         compiler_params=remote(0),
         name="exchange",
-    )(packed, viscosity, log_friction)
+    )(packed, *eq_edges)
     meta = got[:, cap, 0, :].astype(jnp.int32).reshape(devices * 128)
-    forcing = pl.pallas_call(
+    forcing, *f_edges = pl.pallas_call(
         functools.partial(scatter_kernel, cap, cols // seg),
-        out_shape=jax.ShapeDtypeStruct((2, rows, cols), f32),
+        out_shape=[jax.ShapeDtypeStruct((2, rows, cols), f32)] + edge_shapes,
         in_specs=[SMEM, VMEM],
-        out_specs=VMEM,
+        out_specs=[VMEM] * 5,
         compiler_params=params,
         name="scatter",
     )(meta, got)
     f_halo = pl.pallas_call(
         edge_kernel,
-        out_shape=[jax.ShapeDtypeStruct((2,) + shape, f32) for shape in halo],
-        in_specs=[ANY],
-        out_specs=[VMEM] * 4,
+        out_shape=halo_shapes,
+        in_specs=[VMEM] * 4,
+        out_specs=[VMEM] * 5,
         scratch_shapes=[pltpu.SemaphoreType.DMA((8,)), pltpu.SemaphoreType.DMA((8,))],
         compiler_params=remote(1),
         name="edges",
-    )(forcing)
+    )(*f_edges)
     coarse_rows = rows // CB
     big = (rows + 2 * R0, cols + 2 * CH)
     adjoint, coarse = pl.pallas_call(
@@ -448,7 +520,7 @@
             jax.ShapeDtypeStruct((2, rows, cols), f32),
             jax.ShapeDtypeStruct((tiles_x, coarse_rows // tiles_x, cols // CB), f32),
         ),
-        in_specs=[ANY] * 16,
+        in_specs=[ANY] + [VMEM] * 5 + [ANY] * 2 + [VMEM] * 5 + [ANY],
         out_specs=(VMEM, VMEM),
         scratch_shapes=[
             pltpu.VMEM((2,) + big, f32),
@@ -459,7 +531,7 @@
             pltpu.VMEM((2,) + big, f32),
             pltpu.VMEM((2, rows, cols), f32),
             pltpu.VMEM((coarse_rows * 8, cols), f32),
-            pltpu.SemaphoreType.DMA((21,)),
+            pltpu.SemaphoreType.DMA((5,)),
         ],
         compiler_params=params,
         name="stencil",

time: 148 us -> 145 us (0.980)
  Pallas kernels: 144 us -> 141 us
    pallas_call x2, Pallas kernels: 30.1 us -> 45.2 us  [the longest x1 35.8 us: shards(): pl.pallas_call(edge_kernel, out_shape=halo_shapes, in_specs=[VMEM] * 4, o...]
    pallas_call x1, Pallas kernels: 23.2 us -> 10.8 us  [shards(): pl.pallas_call(functools.partial(scatter_kernel, cap, cols // seg), out_s...]
    pallas_call x1, Pallas kernels: 11.2 us -> 6.04 us  [shards(): pl.pallas_call(coarse_kernel, out_shape=jax.ShapeDtypeStruct((coarse_rows...]
where the time goes in v3:
time: 145 us; the launch traced here: 144 us
  Pallas kernels  141 us (97%)
  other arithmetic  1.45 us (1%)
    pallas_call x1, Pallas kernels, shards(): pl.pallas_call(exchange_kernel, out_shape=[jax.ShapeDtypeStruct(packed.sh...  49.4 us
    pallas_call x1, Pallas kernels, shards(): pl.pallas_call(edge_kernel, out_shape=halo_shapes, in_specs=[VMEM] * 4, o...  35.8 us
    pallas_call x1, Pallas kernels, shards(): pl.pallas_call(stencil_kernel, out_shape=(jax.ShapeDtypeStruct((2, rows,...  29.6 us
    pallas_call x1, Pallas kernels, shards(): pl.pallas_call(functools.partial(scatter_kernel, cap, cols // seg), out_s...  10.8 us
    pallas_call x1, Pallas kernels, shards(): pl.pallas_call(functools.partial(pack_kernel, cap), out_shape=[jax.ShapeD...  9.39 us
    pallas_call x1, Pallas kernels, shards(): pl.pallas_call(coarse_kernel, out_shape=jax.ShapeDtypeStruct((coarse_rows...  6.04 us

profile of v3, /device:TPU:0, one launch (start us, length us, event | category | flops | bytes accessed | tf_op | source)
XLA Modules:
  0.0 144.4 jit_solution(6643913400030492753)
XLA Ops:
  0.6 9.4 %pack.1 = (f32[32,33,4,128]{3,2,1,0:T(4,128)}, f32[8,2048]{1,0:T(8,128)}, f32[8,2048]{1,0:T(8,128)}, f32[8,256]{1,0:T(8,128)}, f32[8,256]{1,0:T(8,128)}) custom-call(s32[512]{0:T(512)} %bitcast.9, s32[512]{0:T(512)} %slot_ref.1, f32[512,4,128]{2,1,0:T(4,128)} %bitcast.7, f32[256,2048]{1,0:T(8,128)} %eta_in.3, f32[256,2048]{1,0:T(8,128)} %q_in.3), custom_call_target="tpu_custom_call" | custom-call | tf_op jit(solution)/shard_map/pack/pallas_call | solution.py:462
  10.0 49.4 %exchange.1 = (f32[32,33,4,128]{3,2,1,0:T(4,128)}, f32[8,2048]{1,0:T(8,128)}, f32[8,2048]{1,0:T(8,128)}, f32[8,256]{1,0:T(8,128)}, f32[8,256]{1,0:T(8,128)}, /*index=5*/f32[4,8,128]{2,1,0:T(8,128)}) custom-call(f32[32,33,4,128]{3,2,1,0:T(4,128)} %get-tuple-element.25.packed, f32[8,2048]{1,0:T(8,128)} %get-tuple-element.26.north, ...), custom_call_target="tpu_custom_call" | custom-call | tf_op jit(solution)/shard_map/exchange/pallas_call | solution.py:482
  59.5 1.5 %slice_convert_fusion = s32[32,1,1,128]{3,2,1,0:T(1,128)} fusion(f32[32,33,4,128]{3,2,1,0:T(4,128)} %get-tuple-element.30.got_ref), kind=kLoop, calls=%fused_computation | loop fusion | flops 4096 | bytes 32768 | tf_op jit(solution)/shard_map/convert_element_type | solution.py:497
  60.9 10.8 %scatter.1 = (f32[2,256,2048]{2,1,0:T(8,128)}, f32[8,2048]{1,0:T(8,128)}, f32[8,2048]{1,0:T(8,128)}, f32[8,256]{1,0:T(8,128)}, f32[8,256]{1,0:T(8,128)}) custom-call(s32[4096]{0:T(1024)} %bitcast.8, f32[32,33,4,128]{3,2,1,0:T(4,128)} %get-tuple-element.30.got_ref), custom_call_target="tpu_custom_call" | custom-call | tf_op jit(solution)/shard_map/scatter/pallas_call | solution.py:498
  71.7 35.8 %edges.1 = (f32[8,2048]{1,0:T(8,128)}, f32[8,2048]{1,0:T(8,128)}, f32[8,256]{1,0:T(8,128)}, f32[8,256]{1,0:T(8,128)}, f32[4,8,128]{2,1,0:T(8,128)}) custom-call(f32[8,2048]{1,0:T(8,128)} %get-tuple-element.32.north, f32[8,2048]{1,0:T(8,128)} %get-tuple-element.33.south, f32[8,256]{1,0:T(8,128)} %get-tuple-element.34.west, f32[8,256]{1,0:T(8,128)} %get-tuple-element.35.east), custom_call_target="tpu_custom_call" | custom-call | tf_op jit(solution)/shard_map/edges/pallas_call | solution.py:506
  107.5 29.6 %stencil.1 = (f32[2,256,2048]{2,1,0:T(8,128)}, f32[8,2,128]{2,1,0:T(2,128)}) custom-call(f32[2,256,2048]{2,1,0:T(8,128)} %get-tuple-element.31.f_in, f32[8,2048]{1,0:T(8,128)} %get-tuple-element.36.ft, f32[8,2048]{1,0:T(8,128)} %get-tuple-element.37.fb, f32[8,256]{1,0:T(8,128)} %get-tuple-element.38.fl, f32[8,256]{1,0:T(8,128)} %get-tuple-element.39.fr, ...), custom_call_target="tpu_custom_call" | custom-call | tf_op jit(solution)/shard_map/stencil/pallas_call | solution.py:517
  137.1 6.0 %coarse.1 = f32[2,1024]{1,0:T(2,128)} custom-call(f32[8,2,128]{2,1,0:T(2,128)} %get-tuple-element.47.part), custom_call_target="tpu_custom_call" | custom-call | tf_op jit(solution)/shard_map/coarse/pallas_call | solution.py:539
  143.1 1.3 copy.10

commit v4 on v3

--- a/solution.py
+++ b/solution.py
@@ -64,7 +64,7 @@
         out_ref[t, cap] = jnp.where(lanes == r, slot, jnp.where(lanes == cap, filled, head))
         return carry
 
-    lax.fori_loop(0, rows_ref.shape[0], place, 0)
+    lax.fori_loop(0, rows_ref.shape[0], place, 0, unroll=4)
     for copy in copies:
         copy.wait()
     fields = [
@@ -75,27 +75,44 @@
         ref[...] = value
 
 
-def scatter_kernel(cap, segs, meta_ref, got_ref, out_ref, north, south, west, east):
+def scatter_kernel(cap, segs, meta_ref, got_ref, out_ref, north, south, west, east, second):
     out_ref[...] = jnp.zeros_like(out_ref)
     lanes = lax.broadcasted_iota(jnp.int32, (8, 128), 0)
 
+    second[...] = jnp.zeros_like(second)
+    step = 4 if cap % 4 == 0 else 2 if cap % 2 == 0 else 1
+
     def source(s, carry):
-        def add(r, inner):
-            slot = meta_ref[s * 128 + r]
-            y = slot // segs
-            x = pl.multiple_of((slot % segs) * 256, 256)
-            base = pl.multiple_of(y // 8 * 8, 8)
-            chosen = lanes == y % 8
-            spots = [(c, pl.ds(base, 8), pl.ds(x + 128 * h, 128)) for h in range(2) for c in range(2)]
-            olds = [out_ref[spot] for spot in spots]
-            news = [got_ref[s, r, pl.ds(j, 1), :] for j in range(4)]
-            for spot, old, new in zip(spots, olds, news):
-                out_ref[spot] = old + jnp.where(chosen, new, 0.0)
+        filled = meta_ref[s * 128 + cap]
+
+        def add(k, inner):
+            spots, news = [], []
+            for i in range(step):
+                r = k * step + i
+                slot = meta_ref[s * 128 + r]
+                y = slot // segs
+                x = pl.multiple_of((slot - y * segs) * 256, 256)
+                base = pl.multiple_of(y // 8 * 8, 8)
+                chosen = lanes == jnp.where(r < filled, y - base, -1)
+                spots.append(
+                    [(c, pl.ds(base, 8), pl.ds(x + 128 * h, 128)) for h in range(2) for c in range(2)]
+                )
+                row = [got_ref[s, r, pl.ds(j, 1), :] for j in range(4)]
+                news.append([jnp.where(chosen, part, 0.0) for part in row])
+            for i in range(0, step, 2):
+                pairs = list(zip((out_ref, second), spots[i : i + 2], news[i : i + 2]))
+                sums = [
+                    [ref[spot] + new for spot, new in zip(where, what)] for ref, where, what in pairs
+                ]
+                for (ref, where, _), values in zip(pairs, sums):
+                    for spot, value in zip(where, values):
+                        ref[spot] = value
             return inner
 
-        return lax.fori_loop(0, meta_ref[s * 128 + cap], add, carry)
+        return lax.fori_loop(0, (filled + step - 1) // step, add, carry)
 
     lax.fori_loop(0, got_ref.shape[0], source, 0)
+    out_ref[...] += second[...]
     _, rows, cols = out_ref.shape
     fields = [
         (
@@ -339,13 +356,15 @@
     send, recv, edge_send, edge_recv, local,
 ):
     devices = packed.shape[0]
-    ntx = lax.axis_size("tx")
+    nty, ntx = lax.axis_size("ty"), lax.axis_size("tx")
     me = lax.axis_index("ty") * ntx + lax.axis_index("tx")
     barrier = pltpu.get_barrier_semaphore()
 
     def place(d):
-        target = lax.rem(me + d, devices)
-        return target, (target // ntx, lax.rem(target, ntx))
+        turn = lax.rem(d + nty // 2, devices)
+        y = lax.rem(lax.axis_index("ty") + nty + nty // 2 - lax.rem(turn, nty), nty)
+        x = lax.rem(lax.axis_index("tx") + turn // nty, ntx)
+        return y * ntx + x, (y, x)
 
     def greet(d, carry):
         pl.semaphore_signal(
@@ -500,6 +519,7 @@
         out_shape=[jax.ShapeDtypeStruct((2, rows, cols), f32)] + edge_shapes,
         in_specs=[SMEM, VMEM],
         out_specs=[VMEM] * 5,
+        scratch_shapes=[pltpu.VMEM((2, rows, cols), f32)],
         compiler_params=params,
         name="scatter",
     )(meta, got)

time: 145 us -> 134 us (0.924)
  Pallas kernels: 141 us -> 130 us
    pallas_call x1, Pallas kernels: 35.8 us -> 10.4 us  [shards(): pl.pallas_call(edge_kernel, out_shape=halo_shapes, in_specs=[VMEM] * 4, o...]
    pallas_call x1, Pallas kernels: 49.4 us -> 57.9 us  [shards(): pl.pallas_call(exchange_kernel, out_shape=[jax.ShapeDtypeStruct(packed.sh...]
    pallas_call x1, Pallas kernels: 10.8 us -> 15.3 us  [shards(): pl.pallas_call(functools.partial(scatter_kernel, cap, cols // seg), out_s...]
    pallas_call x1, Pallas kernels: 6.04 us -> 10.2 us  [shards(): pl.pallas_call(coarse_kernel, out_shape=jax.ShapeDtypeStruct((coarse_rows...]
    pallas_call x1, Pallas kernels: 9.39 us -> 6.42 us  [shards(): pl.pallas_call(functools.partial(pack_kernel, cap), out_shape=[jax.ShapeD...]
where the time goes in v4:
time: 134 us; the launch traced here: 133 us
  Pallas kernels  130 us (97%)
  other arithmetic  1.45 us (1%)
    pallas_call x1, Pallas kernels, shards(): pl.pallas_call(exchange_kernel, out_shape=[jax.ShapeDtypeStruct(packed.sh...  57.9 us
    pallas_call x1, Pallas kernels, shards(): pl.pallas_call(stencil_kernel, out_shape=(jax.ShapeDtypeStruct((2, rows,...  29.6 us
    pallas_call x1, Pallas kernels, shards(): pl.pallas_call(functools.partial(scatter_kernel, cap, cols // seg), out_s...  15.3 us
    pallas_call x1, Pallas kernels, shards(): pl.pallas_call(edge_kernel, out_shape=halo_shapes, in_specs=[VMEM] * 4, o...  10.4 us
    pallas_call x1, Pallas kernels, shards(): pl.pallas_call(coarse_kernel, out_shape=jax.ShapeDtypeStruct((coarse_rows...  10.2 us
    pallas_call x1, Pallas kernels, shards(): pl.pallas_call(functools.partial(pack_kernel, cap), out_shape=[jax.ShapeD...  6.42 us

profile of v4, /device:TPU:0, one launch (start us, length us, event | category | flops | bytes accessed | tf_op | source)
XLA Modules:
  0.0 133.2 jit_solution(5834784883154211762)
XLA Ops:
  0.6 6.4 %pack.1 = (f32[32,33,4,128]{3,2,1,0:T(4,128)}, f32[8,2048]{1,0:T(8,128)}, f32[8,2048]{1,0:T(8,128)}, f32[8,256]{1,0:T(8,128)}, f32[8,256]{1,0:T(8,128)}) custom-call(s32[512]{0:T(512)} %bitcast.9, s32[512]{0:T(512)} %slot_ref.1, f32[512,4,128]{2,1,0:T(4,128)} %bitcast.7, f32[256,2048]{1,0:T(8,128)} %eta_in.3, f32[256,2048]{1,0:T(8,128)} %q_in.3), custom_call_target="tpu_custom_call" | custom-call | tf_op jit(solution)/shard_map/pack/pallas_call | solution.py:481
  7.1 57.9 %exchange.1 = (f32[32,33,4,128]{3,2,1,0:T(4,128)}, f32[8,2048]{1,0:T(8,128)}, f32[8,2048]{1,0:T(8,128)}, f32[8,256]{1,0:T(8,128)}, f32[8,256]{1,0:T(8,128)}, /*index=5*/f32[4,8,128]{2,1,0:T(8,128)}) custom-call(f32[32,33,4,128]{3,2,1,0:T(4,128)} %get-tuple-element.25.packed, f32[8,2048]{1,0:T(8,128)} %get-tuple-element.26.north, ...), custom_call_target="tpu_custom_call" | custom-call | tf_op jit(solution)/shard_map/exchange/pallas_call | solution.py:501
  65.0 1.5 %slice_convert_fusion = s32[32,1,1,128]{3,2,1,0:T(1,128)} fusion(f32[32,33,4,128]{3,2,1,0:T(4,128)} %get-tuple-element.30.got_ref), kind=kLoop, calls=%fused_computation | loop fusion | flops 4096 | bytes 32768 | tf_op jit(solution)/shard_map/convert_element_type | solution.py:516
  66.4 15.3 %scatter.1 = (f32[2,256,2048]{2,1,0:T(8,128)}, f32[8,2048]{1,0:T(8,128)}, f32[8,2048]{1,0:T(8,128)}, f32[8,256]{1,0:T(8,128)}, f32[8,256]{1,0:T(8,128)}) custom-call(s32[4096]{0:T(1024)} %bitcast.8, f32[32,33,4,128]{3,2,1,0:T(4,128)} %get-tuple-element.30.got_ref), custom_call_target="tpu_custom_call" | custom-call | tf_op jit(solution)/shard_map/scatter/pallas_call | solution.py:517
  81.7 10.4 %edges.1 = (f32[8,2048]{1,0:T(8,128)}, f32[8,2048]{1,0:T(8,128)}, f32[8,256]{1,0:T(8,128)}, f32[8,256]{1,0:T(8,128)}, f32[4,8,128]{2,1,0:T(8,128)}) custom-call(f32[8,2048]{1,0:T(8,128)} %get-tuple-element.32.north, f32[8,2048]{1,0:T(8,128)} %get-tuple-element.33.south, f32[8,256]{1,0:T(8,128)} %get-tuple-element.34.west, f32[8,256]{1,0:T(8,128)} %get-tuple-element.35.east), custom_call_target="tpu_custom_call" | custom-call | tf_op jit(solution)/shard_map/edges/pallas_call | solution.py:526
  92.1 29.6 %stencil.1 = (f32[2,256,2048]{2,1,0:T(8,128)}, f32[8,2,128]{2,1,0:T(2,128)}) custom-call(f32[2,256,2048]{2,1,0:T(8,128)} %get-tuple-element.31.f_in, f32[8,2048]{1,0:T(8,128)} %get-tuple-element.36.ft, f32[8,2048]{1,0:T(8,128)} %get-tuple-element.37.fb, f32[8,256]{1,0:T(8,128)} %get-tuple-element.38.fl, f32[8,256]{1,0:T(8,128)} %get-tuple-element.39.fr, ...), custom_call_target="tpu_custom_call" | custom-call | tf_op jit(solution)/shard_map/stencil/pallas_call | solution.py:537
  121.7 10.2 %coarse.1 = f32[2,1024]{1,0:T(2,128)} custom-call(f32[8,2,128]{2,1,0:T(2,128)} %get-tuple-element.47.part), custom_call_target="tpu_custom_call" | custom-call | tf_op jit(solution)/shard_map/coarse/pallas_call | solution.py:559
  131.9 1.3 copy.10

commit v5 on v4

--- a/solution.py
+++ b/solution.py
@@ -80,7 +80,8 @@
     lanes = lax.broadcasted_iota(jnp.int32, (8, 128), 0)
 
     second[...] = jnp.zeros_like(second)
-    step = 4 if cap % 4 == 0 else 2 if cap % 2 == 0 else 1
+    step = 8 if cap % 8 == 0 else 2 if cap % 2 == 0 else 1
+    shift = segs.bit_length() - 1 if segs & (segs - 1) == 0 else None
 
     def source(s, carry):
         filled = meta_ref[s * 128 + cap]
@@ -90,9 +91,9 @@
             for i in range(step):
                 r = k * step + i
                 slot = meta_ref[s * 128 + r]
-                y = slot // segs
+                y = slot // segs if shift is None else slot >> shift
                 x = pl.multiple_of((slot - y * segs) * 256, 256)
-                base = pl.multiple_of(y // 8 * 8, 8)
+                base = pl.multiple_of((y >> 3) * 8, 8)
                 chosen = lanes == jnp.where(r < filled, y - base, -1)
                 spots.append(
                     [(c, pl.ds(base, 8), pl.ds(x + 128 * h, 128)) for h in range(2) for c in range(2)]
@@ -109,7 +110,7 @@
                         ref[spot] = value
             return inner
 
-        return lax.fori_loop(0, (filled + step - 1) // step, add, carry)
+        return lax.fori_loop(0, lax.div(filled + step - 1, step), add, carry)
 
     lax.fori_loop(0, got_ref.shape[0], source, 0)
     out_ref[...] += second[...]

time: 134 us -> 125 us (0.933)
  Pallas kernels: 130 us -> 121 us
    pallas_call x1, Pallas kernels: 15.3 us -> 8.98 us  [shards(): pl.pallas_call(functools.partial(scatter_kernel, cap, cols // seg), out_s...]
    pallas_call x1, Pallas kernels: 10.2 us -> 6.32 us  [shards(): pl.pallas_call(coarse_kernel, out_shape=jax.ShapeDtypeStruct((coarse_rows...]
    pallas_call x1, Pallas kernels: 10.4 us -> 12 us  [shards(): pl.pallas_call(edge_kernel, out_shape=halo_shapes, in_specs=[VMEM] * 4, o...]
where the time goes in v5:
time: 125 us
  Pallas kernels  121 us (97%)
  other arithmetic  1.45 us (1%)
  local copies, waits for them, and re-layouts  1.3 us (1%)
    pallas_call x1, Pallas kernels, shards(): pl.pallas_call(exchange_kernel, out_shape=[jax.ShapeDtypeStruct(packed.sh...  57.9 us
    pallas_call x1, Pallas kernels, shards(): pl.pallas_call(stencil_kernel, out_shape=(jax.ShapeDtypeStruct((2, rows,...  29.6 us
    pallas_call x1, Pallas kernels, shards(): pl.pallas_call(edge_kernel, out_shape=halo_shapes, in_specs=[VMEM] * 4, o...  12 us
    pallas_call x1, Pallas kernels, shards(): pl.pallas_call(functools.partial(scatter_kernel, cap, cols // seg), out_s...  8.98 us
    pallas_call x1, Pallas kernels, shards(): pl.pallas_call(functools.partial(pack_kernel, cap), out_shape=[jax.ShapeD...  6.43 us
    pallas_call x1, Pallas kernels, shards(): pl.pallas_call(coarse_kernel, out_shape=jax.ShapeDtypeStruct((coarse_rows...  6.32 us

profile of v5, /device:TPU:0, one launch (start us, length us, event | category | flops | bytes accessed | tf_op | source)
XLA Modules:
  0.0 124.6 jit_solution(2323541941537995671)
XLA Ops:
  0.6 6.4 %pack.1 = (f32[32,33,4,128]{3,2,1,0:T(4,128)}, f32[8,2048]{1,0:T(8,128)}, f32[8,2048]{1,0:T(8,128)}, f32[8,256]{1,0:T(8,128)}, f32[8,256]{1,0:T(8,128)}) custom-call(s32[512]{0:T(512)} %bitcast.9, s32[512]{0:T(512)} %slot_ref.1, f32[512,4,128]{2,1,0:T(4,128)} %bitcast.7, f32[256,2048]{1,0:T(8,128)} %eta_in.3, f32[256,2048]{1,0:T(8,128)} %q_in.3), custom_call_target="tpu_custom_call" | custom-call | tf_op jit(solution)/shard_map/pack/pallas_call | solution.py:482
  7.1 57.9 %exchange.1 = (f32[32,33,4,128]{3,2,1,0:T(4,128)}, f32[8,2048]{1,0:T(8,128)}, f32[8,2048]{1,0:T(8,128)}, f32[8,256]{1,0:T(8,128)}, f32[8,256]{1,0:T(8,128)}, /*index=5*/f32[4,8,128]{2,1,0:T(8,128)}) custom-call(f32[32,33,4,128]{3,2,1,0:T(4,128)} %get-tuple-element.25.packed, f32[8,2048]{1,0:T(8,128)} %get-tuple-element.26.north, ...), custom_call_target="tpu_custom_call" | custom-call | tf_op jit(solution)/shard_map/exchange/pallas_call | solution.py:502
  65.0 1.5 %slice_convert_fusion = s32[32,1,1,128]{3,2,1,0:T(1,128)} fusion(f32[32,33,4,128]{3,2,1,0:T(4,128)} %get-tuple-element.30.got_ref), kind=kLoop, calls=%fused_computation | loop fusion | flops 4096 | bytes 32768 | tf_op jit(solution)/shard_map/convert_element_type | solution.py:517
  66.4 9.0 %scatter.1 = (f32[2,256,2048]{2,1,0:T(8,128)}, f32[8,2048]{1,0:T(8,128)}, f32[8,2048]{1,0:T(8,128)}, f32[8,256]{1,0:T(8,128)}, f32[8,256]{1,0:T(8,128)}) custom-call(s32[4096]{0:T(1024)} %bitcast.8, f32[32,33,4,128]{3,2,1,0:T(4,128)} %get-tuple-element.30.got_ref), custom_call_target="tpu_custom_call" | custom-call | tf_op jit(solution)/shard_map/scatter/pallas_call | solution.py:518
  75.4 12.0 %edges.1 = (f32[8,2048]{1,0:T(8,128)}, f32[8,2048]{1,0:T(8,128)}, f32[8,256]{1,0:T(8,128)}, f32[8,256]{1,0:T(8,128)}, f32[4,8,128]{2,1,0:T(8,128)}) custom-call(f32[8,2048]{1,0:T(8,128)} %get-tuple-element.32.north, f32[8,2048]{1,0:T(8,128)} %get-tuple-element.33.south, f32[8,256]{1,0:T(8,128)} %get-tuple-element.34.west, f32[8,256]{1,0:T(8,128)} %get-tuple-element.35.east), custom_call_target="tpu_custom_call" | custom-call | tf_op jit(solution)/shard_map/edges/pallas_call | solution.py:527
  87.4 29.6 %stencil.1 = (f32[2,256,2048]{2,1,0:T(8,128)}, f32[8,2,128]{2,1,0:T(2,128)}) custom-call(f32[2,256,2048]{2,1,0:T(8,128)} %get-tuple-element.31.f_in, f32[8,2048]{1,0:T(8,128)} %get-tuple-element.36.ft, f32[8,2048]{1,0:T(8,128)} %get-tuple-element.37.fb, f32[8,256]{1,0:T(8,128)} %get-tuple-element.38.fl, f32[8,256]{1,0:T(8,128)} %get-tuple-element.39.fr, ...), custom_call_target="tpu_custom_call" | custom-call | tf_op jit(solution)/shard_map/stencil/pallas_call | solution.py:538
  117.0 6.3 %coarse.1 = f32[2,1024]{1,0:T(2,128)} custom-call(f32[8,2,128]{2,1,0:T(2,128)} %get-tuple-element.47.part), custom_call_target="tpu_custom_call" | custom-call | tf_op jit(solution)/shard_map/coarse/pallas_call | solution.py:560
  123.3 1.3 %copy.10 = f32[2,1024]{1,0:T(2,128)} copy(f32[2,1024]{1,0:T(2,128)} %coarse.1) | data formatting | bytes 16384
